TPU v7x, 256 devices: a whole 4x4x8 slice. The times are simulated.
256 devices in a mesh: blk: 32 (over y_hi, z, core), rep: 8 (over x, y_lo).
Axes of the slice: x: 4, y: 4 (y_hi: 2, y_lo: 2; y = y_hi * 2 + y_lo), z: 8, core: 2. Of those that a mesh axis runs over, the one named last changes fastest.
Arguments:
- amplitudes: float32 [512, 512, 1024], P('blk', 'rep'), may hold values from -6 to 6
- integrals: float32 [512, 512, 4, 512], P('blk', 'rep'), may hold values from -0.01171875 to 0.01171875
- occ_energy: float32 [64], replicated, may hold values from -2 to -0.5
- virt_energy: float32 [512], replicated, may hold values from 0.3 to 3
- outer_energy: float32 [4], replicated, may hold values from 0.3 to 3
Outputs:
- update: float32 [1024, 2048], P('blk', 'rep')
All inputs are finite; a program needn't handle non-finite values.
Results may differ from a plain program's by a relative error of at most 0.00028.
Values sent between devices are 32-bit elements; how exact they have to be, the bound alone decides.
A program may use at most 64 MiB of HBM per device.

v0:
```python
import jax
import jax.numpy as jnp
from jax import lax
from jax.sharding import PartitionSpec as P

NOCC = 64
NV = 512
A_OUT = 4
I_ROWS = 16


def passed_along(block, axis, distance):
    devices = range(lax.axis_size(axis))
    route = [((i - distance) % len(devices), i) for i in devices]
    return lax.ppermute(block, axis, route)


def contract(tmat, wmat, start, count):
    columns = lax.dynamic_slice_in_dim(tmat, start, count, 1)
    return lax.dot_general(
        columns,
        wmat,
        (((0,), (0,)), ((), ())),
        precision=lax.Precision.HIGHEST,
        preferred_element_type=jnp.float32,
    )


def shards(amplitudes, integrals, occ_energy, virt_energy, outer_energy):
    inner = amplitudes.shape[0] * amplitudes.shape[1]
    pairs = amplitudes.shape[2]
    tmat = amplitudes.reshape(inner, pairs)
    wmat = integrals.reshape(inner, integrals.shape[2] * integrals.shape[3])
    count_blk = lax.axis_size("blk")
    pair_rows = pairs // count_blk
    my_blk = lax.axis_index("blk")
    first = contract(tmat, wmat, (my_blk + count_blk - 1) % count_blk * pair_rows, pair_rows)

    def advance(step, carried):
        carried = passed_along(carried, "blk", 1)
        block = (my_blk + 2 * count_blk - 2 - step) % count_blk
        return carried + contract(tmat, wmat, block * pair_rows, pair_rows)

    carried = lax.fori_loop(0, count_blk - 1, advance, first)
    summed = lax.psum_scatter(carried, "rep", scatter_dimension=1, tiled=True)
    col_rows = summed.shape[1]
    pair_energy = jnp.repeat(occ_energy[:I_ROWS], NOCC) + jnp.tile(occ_energy, I_ROWS)
    column_energy = jnp.repeat(outer_energy, NV) + jnp.tile(virt_energy, A_OUT)
    mine_pairs = lax.dynamic_slice_in_dim(pair_energy, my_blk * pair_rows, pair_rows, 0)
    mine_cols = lax.dynamic_slice_in_dim(
        column_energy, lax.axis_index("rep") * col_rows, col_rows, 0
    )
    return summed / (mine_cols[None, :] - mine_pairs[:, None])


def solution(mesh):
    placed = (P("blk", "rep", None), P("blk", "rep", None, None), P(), P(), P())
    return jax.shard_map(
        shards, mesh=mesh, in_specs=placed, out_specs=P("blk", "rep"), check_vma=False
    )
```

profile of v0, /device:TPU:2, one launch (start us, length us, event | category | flops | bytes accessed | tf_op | source)
XLA Modules:
  0.0 597.9 jit_solution(13006160123885762930)
XLA Ops:
  6.5 10.7 %copy.6 = f32[128,8,4,512]{3,1,2,0:T(8,128)} copy(f32[128,8,4,512]{3,2,1,0:T(4,128)} %bitcast.14) | data formatting | bytes 16777216
  24.8 532.0 %while.15 = (s32[]{:T(128)}, f32[32,2048]{1,0:T(8,128)S(1)}, s32[]{:T(128)}, f32[1024,1024]{1,0:T(8,128)}, f32[1024,2048]{1,0:T(8,128)}, /*index=5*/s32[]{:T(128)}, s32[]{:T(128)}, s32[]{:T(128)}, s32[]{:T(128)}, s32[]{:T(128)}) while((s32[]{:T(128)}, f32[32,2048]{1,0:T(8,128)S(1)}, s32[]{:T(128)}, f32[1024,1024]{1,0:T(8,128)}, ...), condition=%wide.region_1.2_spmd, body=%wide.region_0.1_spmd.sunk | while | flops 805371904 | bytes 10486072 | solution.py:44
  25.0 11.9 %collective-permute-done = f32[32,2048]{1,0:T(8,128)S(1)} collective-permute-done((f32[32,2048]{1,0:T(8,128)S(1)}, f32[32,2048]{1,0:T(8,128)S(1)}, u32[]{:S(2)}, u32[]{:S(2)}) %collective-permute-start) | collective-permute-done | bytes 262176 | tf_op jit(solution)/shard_map/while/body/eval_jaxpr/ppermute | solution.py:15
  44.6 9.4 %collective-permute-done = f32[32,2048]{1,0:T(8,128)S(1)} collective-permute-done((f32[32,2048]{1,0:T(8,128)S(1)}, f32[32,2048]{1,0:T(8,128)S(1)}, u32[]{:S(2)}, u32[]{:S(2)}) %collective-permute-start) | collective-permute-done | bytes 262176 | tf_op jit(solution)/shard_map/while/body/eval_jaxpr/ppermute | solution.py:15
  61.7 9.4 %collective-permute-done = f32[32,2048]{1,0:T(8,128)S(1)} collective-permute-done((f32[32,2048]{1,0:T(8,128)S(1)}, f32[32,2048]{1,0:T(8,128)S(1)}, u32[]{:S(2)}, u32[]{:S(2)}) %collective-permute-start) | collective-permute-done | bytes 262176 | tf_op jit(solution)/shard_map/while/body/eval_jaxpr/ppermute | solution.py:15
  78.8 9.4 %collective-permute-done = f32[32,2048]{1,0:T(8,128)S(1)} collective-permute-done((f32[32,2048]{1,0:T(8,128)S(1)}, f32[32,2048]{1,0:T(8,128)S(1)}, u32[]{:S(2)}, u32[]{:S(2)}) %collective-permute-start) | collective-permute-done | bytes 262176 | tf_op jit(solution)/shard_map/while/body/eval_jaxpr/ppermute | solution.py:15
  95.8 9.4 %collective-permute-done = f32[32,2048]{1,0:T(8,128)S(1)} collective-permute-done((f32[32,2048]{1,0:T(8,128)S(1)}, f32[32,2048]{1,0:T(8,128)S(1)}, u32[]{:S(2)}, u32[]{:S(2)}) %collective-permute-start) | collective-permute-done | bytes 262176 | tf_op jit(solution)/shard_map/while/body/eval_jaxpr/ppermute | solution.py:15
  112.9 9.4 %collective-permute-done = f32[32,2048]{1,0:T(8,128)S(1)} collective-permute-done((f32[32,2048]{1,0:T(8,128)S(1)}, f32[32,2048]{1,0:T(8,128)S(1)}, u32[]{:S(2)}, u32[]{:S(2)}) %collective-permute-start) | collective-permute-done | bytes 262176 | tf_op jit(solution)/shard_map/while/body/eval_jaxpr/ppermute | solution.py:15
  130.0 9.4 %collective-permute-done = f32[32,2048]{1,0:T(8,128)S(1)} collective-permute-done((f32[32,2048]{1,0:T(8,128)S(1)}, f32[32,2048]{1,0:T(8,128)S(1)}, u32[]{:S(2)}, u32[]{:S(2)}) %collective-permute-start) | collective-permute-done | bytes 262176 | tf_op jit(solution)/shard_map/while/body/eval_jaxpr/ppermute | solution.py:15
  147.1 9.4 %collective-permute-done = f32[32,2048]{1,0:T(8,128)S(1)} collective-permute-done((f32[32,2048]{1,0:T(8,128)S(1)}, f32[32,2048]{1,0:T(8,128)S(1)}, u32[]{:S(2)}, u32[]{:S(2)}) %collective-permute-start) | collective-permute-done | bytes 262176 | tf_op jit(solution)/shard_map/while/body/eval_jaxpr/ppermute | solution.py:15
  164.2 9.4 %collective-permute-done = f32[32,2048]{1,0:T(8,128)S(1)} collective-permute-done((f32[32,2048]{1,0:T(8,128)S(1)}, f32[32,2048]{1,0:T(8,128)S(1)}, u32[]{:S(2)}, u32[]{:S(2)}) %collective-permute-start) | collective-permute-done | bytes 262176 | tf_op jit(solution)/shard_map/while/body/eval_jaxpr/ppermute | solution.py:15
  181.2 9.4 %collective-permute-done = f32[32,2048]{1,0:T(8,128)S(1)} collective-permute-done((f32[32,2048]{1,0:T(8,128)S(1)}, f32[32,2048]{1,0:T(8,128)S(1)}, u32[]{:S(2)}, u32[]{:S(2)}) %collective-permute-start) | collective-permute-done | bytes 262176 | tf_op jit(solution)/shard_map/while/body/eval_jaxpr/ppermute | solution.py:15
  198.3 9.4 %collective-permute-done = f32[32,2048]{1,0:T(8,128)S(1)} collective-permute-done((f32[32,2048]{1,0:T(8,128)S(1)}, f32[32,2048]{1,0:T(8,128)S(1)}, u32[]{:S(2)}, u32[]{:S(2)}) %collective-permute-start) | collective-permute-done | bytes 262176 | tf_op jit(solution)/shard_map/while/body/eval_jaxpr/ppermute | solution.py:15
  215.4 9.4 %collective-permute-done = f32[32,2048]{1,0:T(8,128)S(1)} collective-permute-done((f32[32,2048]{1,0:T(8,128)S(1)}, f32[32,2048]{1,0:T(8,128)S(1)}, u32[]{:S(2)}, u32[]{:S(2)}) %collective-permute-start) | collective-permute-done | bytes 262176 | tf_op jit(solution)/shard_map/while/body/eval_jaxpr/ppermute | solution.py:15
  232.5 9.4 %collective-permute-done = f32[32,2048]{1,0:T(8,128)S(1)} collective-permute-done((f32[32,2048]{1,0:T(8,128)S(1)}, f32[32,2048]{1,0:T(8,128)S(1)}, u32[]{:S(2)}, u32[]{:S(2)}) %collective-permute-start) | collective-permute-done | bytes 262176 | tf_op jit(solution)/shard_map/while/body/eval_jaxpr/ppermute | solution.py:15
  249.5 9.4 %collective-permute-done = f32[32,2048]{1,0:T(8,128)S(1)} collective-permute-done((f32[32,2048]{1,0:T(8,128)S(1)}, f32[32,2048]{1,0:T(8,128)S(1)}, u32[]{:S(2)}, u32[]{:S(2)}) %collective-permute-start) | collective-permute-done | bytes 262176 | tf_op jit(solution)/shard_map/while/body/eval_jaxpr/ppermute | solution.py:15
  266.6 9.4 %collective-permute-done = f32[32,2048]{1,0:T(8,128)S(1)} collective-permute-done((f32[32,2048]{1,0:T(8,128)S(1)}, f32[32,2048]{1,0:T(8,128)S(1)}, u32[]{:S(2)}, u32[]{:S(2)}) %collective-permute-start) | collective-permute-done | bytes 262176 | tf_op jit(solution)/shard_map/while/body/eval_jaxpr/ppermute | solution.py:15
  283.7 9.4 %collective-permute-done = f32[32,2048]{1,0:T(8,128)S(1)} collective-permute-done((f32[32,2048]{1,0:T(8,128)S(1)}, f32[32,2048]{1,0:T(8,128)S(1)}, u32[]{:S(2)}, u32[]{:S(2)}) %collective-permute-start) | collective-permute-done | bytes 262176 | tf_op jit(solution)/shard_map/while/body/eval_jaxpr/ppermute | solution.py:15
  300.8 9.4 %collective-permute-done = f32[32,2048]{1,0:T(8,128)S(1)} collective-permute-done((f32[32,2048]{1,0:T(8,128)S(1)}, f32[32,2048]{1,0:T(8,128)S(1)}, u32[]{:S(2)}, u32[]{:S(2)}) %collective-permute-start) | collective-permute-done | bytes 262176 | tf_op jit(solution)/shard_map/while/body/eval_jaxpr/ppermute | solution.py:15
  317.9 9.4 %collective-permute-done = f32[32,2048]{1,0:T(8,128)S(1)} collective-permute-done((f32[32,2048]{1,0:T(8,128)S(1)}, f32[32,2048]{1,0:T(8,128)S(1)}, u32[]{:S(2)}, u32[]{:S(2)}) %collective-permute-start) | collective-permute-done | bytes 262176 | tf_op jit(solution)/shard_map/while/body/eval_jaxpr/ppermute | solution.py:15
  334.9 9.4 %collective-permute-done = f32[32,2048]{1,0:T(8,128)S(1)} collective-permute-done((f32[32,2048]{1,0:T(8,128)S(1)}, f32[32,2048]{1,0:T(8,128)S(1)}, u32[]{:S(2)}, u32[]{:S(2)}) %collective-permute-start) | collective-permute-done | bytes 262176 | tf_op jit(solution)/shard_map/while/body/eval_jaxpr/ppermute | solution.py:15
  352.0 9.4 %collective-permute-done = f32[32,2048]{1,0:T(8,128)S(1)} collective-permute-done((f32[32,2048]{1,0:T(8,128)S(1)}, f32[32,2048]{1,0:T(8,128)S(1)}, u32[]{:S(2)}, u32[]{:S(2)}) %collective-permute-start) | collective-permute-done | bytes 262176 | tf_op jit(solution)/shard_map/while/body/eval_jaxpr/ppermute | solution.py:15
  369.1 9.4 %collective-permute-done = f32[32,2048]{1,0:T(8,128)S(1)} collective-permute-done((f32[32,2048]{1,0:T(8,128)S(1)}, f32[32,2048]{1,0:T(8,128)S(1)}, u32[]{:S(2)}, u32[]{:S(2)}) %collective-permute-start) | collective-permute-done | bytes 262176 | tf_op jit(solution)/shard_map/while/body/eval_jaxpr/ppermute | solution.py:15
  386.2 9.4 %collective-permute-done = f32[32,2048]{1,0:T(8,128)S(1)} collective-permute-done((f32[32,2048]{1,0:T(8,128)S(1)}, f32[32,2048]{1,0:T(8,128)S(1)}, u32[]{:S(2)}, u32[]{:S(2)}) %collective-permute-start) | collective-permute-done | bytes 262176 | tf_op jit(solution)/shard_map/while/body/eval_jaxpr/ppermute | solution.py:15
  403.2 9.4 %collective-permute-done = f32[32,2048]{1,0:T(8,128)S(1)} collective-permute-done((f32[32,2048]{1,0:T(8,128)S(1)}, f32[32,2048]{1,0:T(8,128)S(1)}, u32[]{:S(2)}, u32[]{:S(2)}) %collective-permute-start) | collective-permute-done | bytes 262176 | tf_op jit(solution)/shard_map/while/body/eval_jaxpr/ppermute | solution.py:15
  420.3 9.4 %collective-permute-done = f32[32,2048]{1,0:T(8,128)S(1)} collective-permute-done((f32[32,2048]{1,0:T(8,128)S(1)}, f32[32,2048]{1,0:T(8,128)S(1)}, u32[]{:S(2)}, u32[]{:S(2)}) %collective-permute-start) | collective-permute-done | bytes 262176 | tf_op jit(solution)/shard_map/while/body/eval_jaxpr/ppermute | solution.py:15
  437.4 9.4 %collective-permute-done = f32[32,2048]{1,0:T(8,128)S(1)} collective-permute-done((f32[32,2048]{1,0:T(8,128)S(1)}, f32[32,2048]{1,0:T(8,128)S(1)}, u32[]{:S(2)}, u32[]{:S(2)}) %collective-permute-start) | collective-permute-done | bytes 262176 | tf_op jit(solution)/shard_map/while/body/eval_jaxpr/ppermute | solution.py:15
  454.5 9.4 %collective-permute-done = f32[32,2048]{1,0:T(8,128)S(1)} collective-permute-done((f32[32,2048]{1,0:T(8,128)S(1)}, f32[32,2048]{1,0:T(8,128)S(1)}, u32[]{:S(2)}, u32[]{:S(2)}) %collective-permute-start) | collective-permute-done | bytes 262176 | tf_op jit(solution)/shard_map/while/body/eval_jaxpr/ppermute | solution.py:15
  471.6 9.4 %collective-permute-done = f32[32,2048]{1,0:T(8,128)S(1)} collective-permute-done((f32[32,2048]{1,0:T(8,128)S(1)}, f32[32,2048]{1,0:T(8,128)S(1)}, u32[]{:S(2)}, u32[]{:S(2)}) %collective-permute-start) | collective-permute-done | bytes 262176 | tf_op jit(solution)/shard_map/while/body/eval_jaxpr/ppermute | solution.py:15
  488.6 9.4 %collective-permute-done = f32[32,2048]{1,0:T(8,128)S(1)} collective-permute-done((f32[32,2048]{1,0:T(8,128)S(1)}, f32[32,2048]{1,0:T(8,128)S(1)}, u32[]{:S(2)}, u32[]{:S(2)}) %collective-permute-start) | collective-permute-done | bytes 262176 | tf_op jit(solution)/shard_map/while/body/eval_jaxpr/ppermute | solution.py:15
  505.7 9.4 %collective-permute-done = f32[32,2048]{1,0:T(8,128)S(1)} collective-permute-done((f32[32,2048]{1,0:T(8,128)S(1)}, f32[32,2048]{1,0:T(8,128)S(1)}, u32[]{:S(2)}, u32[]{:S(2)}) %collective-permute-start) | collective-permute-done | bytes 262176 | tf_op jit(solution)/shard_map/while/body/eval_jaxpr/ppermute | solution.py:15
  557.9 31.6 %reduce-scatter.2.cloned.1.call-done = f32[32,256]{1,0:T(8,128)} async-done(((f32[32,2048]{1,0:T(8,128)}), f32[32,256]{1,0:T(8,128)}) %reduce-scatter.2.cloned.1.call-update) | async-done | bytes 32784 | tf_op jit(solution)/shard_map/reduce_scatter | solution.py:45
  (82 shorter events, 266.0 us)
Async XLA Ops:
  6.5 583.0 %reduce-scatter.2.cloned.1.call-start = ((), (), s32[]{:S(2)}) async-start(), calls=%async_computation.1 | async-start | bytes 294912 | tf_op jit(solution)/shard_map/reduce_scatter | solution.py:45
  24.8 12.1 %collective-permute-start = (f32[32,2048]{1,0:T(8,128)S(1)}, f32[32,2048]{1,0:T(8,128)S(1)}, u32[]{:S(2)}, u32[]{:S(2)}) collective-permute-start(f32[32,2048]{1,0:T(8,128)S(1)} %get-tuple-element.195), channel_id=1, source_target_pairs={{248,0},{0,8},{8,16},{16,24},{24,32},{32,40},{40,48},{48,56},{56,6... | collective-permute-start | bytes 786440 | tf_op jit(solution)/shard_map/while/body/eval_jaxpr/ppermute | solution.py:15
  44.5 9.5 %collective-permute-start = (f32[32,2048]{1,0:T(8,128)S(1)}, f32[32,2048]{1,0:T(8,128)S(1)}, u32[]{:S(2)}, u32[]{:S(2)}) collective-permute-start(f32[32,2048]{1,0:T(8,128)S(1)} %get-tuple-element.195), channel_id=1, source_target_pairs={{248,0},{0,8},{8,16},{16,24},{24,32},{32,40},{40,48},{48,56},{56,6... | collective-permute-start | bytes 786440 | tf_op jit(solution)/shard_map/while/body/eval_jaxpr/ppermute | solution.py:15
  61.6 9.5 %collective-permute-start = (f32[32,2048]{1,0:T(8,128)S(1)}, f32[32,2048]{1,0:T(8,128)S(1)}, u32[]{:S(2)}, u32[]{:S(2)}) collective-permute-start(f32[32,2048]{1,0:T(8,128)S(1)} %get-tuple-element.195), channel_id=1, source_target_pairs={{248,0},{0,8},{8,16},{16,24},{24,32},{32,40},{40,48},{48,56},{56,6... | collective-permute-start | bytes 786440 | tf_op jit(solution)/shard_map/while/body/eval_jaxpr/ppermute | solution.py:15
  78.7 9.5 %collective-permute-start = (f32[32,2048]{1,0:T(8,128)S(1)}, f32[32,2048]{1,0:T(8,128)S(1)}, u32[]{:S(2)}, u32[]{:S(2)}) collective-permute-start(f32[32,2048]{1,0:T(8,128)S(1)} %get-tuple-element.195), channel_id=1, source_target_pairs={{248,0},{0,8},{8,16},{16,24},{24,32},{32,40},{40,48},{48,56},{56,6... | collective-permute-start | bytes 786440 | tf_op jit(solution)/shard_map/while/body/eval_jaxpr/ppermute | solution.py:15
  95.7 9.5 %collective-permute-start = (f32[32,2048]{1,0:T(8,128)S(1)}, f32[32,2048]{1,0:T(8,128)S(1)}, u32[]{:S(2)}, u32[]{:S(2)}) collective-permute-start(f32[32,2048]{1,0:T(8,128)S(1)} %get-tuple-element.195), channel_id=1, source_target_pairs={{248,0},{0,8},{8,16},{16,24},{24,32},{32,40},{40,48},{48,56},{56,6... | collective-permute-start | bytes 786440 | tf_op jit(solution)/shard_map/while/body/eval_jaxpr/ppermute | solution.py:15
  112.8 9.5 %collective-permute-start = (f32[32,2048]{1,0:T(8,128)S(1)}, f32[32,2048]{1,0:T(8,128)S(1)}, u32[]{:S(2)}, u32[]{:S(2)}) collective-permute-start(f32[32,2048]{1,0:T(8,128)S(1)} %get-tuple-element.195), channel_id=1, source_target_pairs={{248,0},{0,8},{8,16},{16,24},{24,32},{32,40},{40,48},{48,56},{56,6... | collective-permute-start | bytes 786440 | tf_op jit(solution)/shard_map/while/body/eval_jaxpr/ppermute | solution.py:15
  129.9 9.5 %collective-permute-start = (f32[32,2048]{1,0:T(8,128)S(1)}, f32[32,2048]{1,0:T(8,128)S(1)}, u32[]{:S(2)}, u32[]{:S(2)}) collective-permute-start(f32[32,2048]{1,0:T(8,128)S(1)} %get-tuple-element.195), channel_id=1, source_target_pairs={{248,0},{0,8},{8,16},{16,24},{24,32},{32,40},{40,48},{48,56},{56,6... | collective-permute-start | bytes 786440 | tf_op jit(solution)/shard_map/while/body/eval_jaxpr/ppermute | solution.py:15
  147.0 9.5 %collective-permute-start = (f32[32,2048]{1,0:T(8,128)S(1)}, f32[32,2048]{1,0:T(8,128)S(1)}, u32[]{:S(2)}, u32[]{:S(2)}) collective-permute-start(f32[32,2048]{1,0:T(8,128)S(1)} %get-tuple-element.195), channel_id=1, source_target_pairs={{248,0},{0,8},{8,16},{16,24},{24,32},{32,40},{40,48},{48,56},{56,6... | collective-permute-start | bytes 786440 | tf_op jit(solution)/shard_map/while/body/eval_jaxpr/ppermute | solution.py:15
  164.0 9.5 %collective-permute-start = (f32[32,2048]{1,0:T(8,128)S(1)}, f32[32,2048]{1,0:T(8,128)S(1)}, u32[]{:S(2)}, u32[]{:S(2)}) collective-permute-start(f32[32,2048]{1,0:T(8,128)S(1)} %get-tuple-element.195), channel_id=1, source_target_pairs={{248,0},{0,8},{8,16},{16,24},{24,32},{32,40},{40,48},{48,56},{56,6... | collective-permute-start | bytes 786440 | tf_op jit(solution)/shard_map/while/body/eval_jaxpr/ppermute | solution.py:15
  181.1 9.5 %collective-permute-start = (f32[32,2048]{1,0:T(8,128)S(1)}, f32[32,2048]{1,0:T(8,128)S(1)}, u32[]{:S(2)}, u32[]{:S(2)}) collective-permute-start(f32[32,2048]{1,0:T(8,128)S(1)} %get-tuple-element.195), channel_id=1, source_target_pairs={{248,0},{0,8},{8,16},{16,24},{24,32},{32,40},{40,48},{48,56},{56,6... | collective-permute-start | bytes 786440 | tf_op jit(solution)/shard_map/while/body/eval_jaxpr/ppermute | solution.py:15
  198.2 9.5 %collective-permute-start = (f32[32,2048]{1,0:T(8,128)S(1)}, f32[32,2048]{1,0:T(8,128)S(1)}, u32[]{:S(2)}, u32[]{:S(2)}) collective-permute-start(f32[32,2048]{1,0:T(8,128)S(1)} %get-tuple-element.195), channel_id=1, source_target_pairs={{248,0},{0,8},{8,16},{16,24},{24,32},{32,40},{40,48},{48,56},{56,6... | collective-permute-start | bytes 786440 | tf_op jit(solution)/shard_map/while/body/eval_jaxpr/ppermute | solution.py:15
  215.3 9.5 %collective-permute-start = (f32[32,2048]{1,0:T(8,128)S(1)}, f32[32,2048]{1,0:T(8,128)S(1)}, u32[]{:S(2)}, u32[]{:S(2)}) collective-permute-start(f32[32,2048]{1,0:T(8,128)S(1)} %get-tuple-element.195), channel_id=1, source_target_pairs={{248,0},{0,8},{8,16},{16,24},{24,32},{32,40},{40,48},{48,56},{56,6... | collective-permute-start | bytes 786440 | tf_op jit(solution)/shard_map/while/body/eval_jaxpr/ppermute | solution.py:15
  232.4 9.5 %collective-permute-start = (f32[32,2048]{1,0:T(8,128)S(1)}, f32[32,2048]{1,0:T(8,128)S(1)}, u32[]{:S(2)}, u32[]{:S(2)}) collective-permute-start(f32[32,2048]{1,0:T(8,128)S(1)} %get-tuple-element.195), channel_id=1, source_target_pairs={{248,0},{0,8},{8,16},{16,24},{24,32},{32,40},{40,48},{48,56},{56,6... | collective-permute-start | bytes 786440 | tf_op jit(solution)/shard_map/while/body/eval_jaxpr/ppermute | solution.py:15
  249.4 9.5 %collective-permute-start = (f32[32,2048]{1,0:T(8,128)S(1)}, f32[32,2048]{1,0:T(8,128)S(1)}, u32[]{:S(2)}, u32[]{:S(2)}) collective-permute-start(f32[32,2048]{1,0:T(8,128)S(1)} %get-tuple-element.195), channel_id=1, source_target_pairs={{248,0},{0,8},{8,16},{16,24},{24,32},{32,40},{40,48},{48,56},{56,6... | collective-permute-start | bytes 786440 | tf_op jit(solution)/shard_map/while/body/eval_jaxpr/ppermute | solution.py:15
  266.5 9.5 %collective-permute-start = (f32[32,2048]{1,0:T(8,128)S(1)}, f32[32,2048]{1,0:T(8,128)S(1)}, u32[]{:S(2)}, u32[]{:S(2)}) collective-permute-start(f32[32,2048]{1,0:T(8,128)S(1)} %get-tuple-element.195), channel_id=1, source_target_pairs={{248,0},{0,8},{8,16},{16,24},{24,32},{32,40},{40,48},{48,56},{56,6... | collective-permute-start | bytes 786440 | tf_op jit(solution)/shard_map/while/body/eval_jaxpr/ppermute | solution.py:15
  283.6 9.5 %collective-permute-start = (f32[32,2048]{1,0:T(8,128)S(1)}, f32[32,2048]{1,0:T(8,128)S(1)}, u32[]{:S(2)}, u32[]{:S(2)}) collective-permute-start(f32[32,2048]{1,0:T(8,128)S(1)} %get-tuple-element.195), channel_id=1, source_target_pairs={{248,0},{0,8},{8,16},{16,24},{24,32},{32,40},{40,48},{48,56},{56,6... | collective-permute-start | bytes 786440 | tf_op jit(solution)/shard_map/while/body/eval_jaxpr/ppermute | solution.py:15
  300.7 9.5 %collective-permute-start = (f32[32,2048]{1,0:T(8,128)S(1)}, f32[32,2048]{1,0:T(8,128)S(1)}, u32[]{:S(2)}, u32[]{:S(2)}) collective-permute-start(f32[32,2048]{1,0:T(8,128)S(1)} %get-tuple-element.195), channel_id=1, source_target_pairs={{248,0},{0,8},{8,16},{16,24},{24,32},{32,40},{40,48},{48,56},{56,6... | collective-permute-start | bytes 786440 | tf_op jit(solution)/shard_map/while/body/eval_jaxpr/ppermute | solution.py:15
  317.7 9.5 %collective-permute-start = (f32[32,2048]{1,0:T(8,128)S(1)}, f32[32,2048]{1,0:T(8,128)S(1)}, u32[]{:S(2)}, u32[]{:S(2)}) collective-permute-start(f32[32,2048]{1,0:T(8,128)S(1)} %get-tuple-element.195), channel_id=1, source_target_pairs={{248,0},{0,8},{8,16},{16,24},{24,32},{32,40},{40,48},{48,56},{56,6... | collective-permute-start | bytes 786440 | tf_op jit(solution)/shard_map/while/body/eval_jaxpr/ppermute | solution.py:15
  334.8 9.5 %collective-permute-start = (f32[32,2048]{1,0:T(8,128)S(1)}, f32[32,2048]{1,0:T(8,128)S(1)}, u32[]{:S(2)}, u32[]{:S(2)}) collective-permute-start(f32[32,2048]{1,0:T(8,128)S(1)} %get-tuple-element.195), channel_id=1, source_target_pairs={{248,0},{0,8},{8,16},{16,24},{24,32},{32,40},{40,48},{48,56},{56,6... | collective-permute-start | bytes 786440 | tf_op jit(solution)/shard_map/while/body/eval_jaxpr/ppermute | solution.py:15
  351.9 9.5 %collective-permute-start = (f32[32,2048]{1,0:T(8,128)S(1)}, f32[32,2048]{1,0:T(8,128)S(1)}, u32[]{:S(2)}, u32[]{:S(2)}) collective-permute-start(f32[32,2048]{1,0:T(8,128)S(1)} %get-tuple-element.195), channel_id=1, source_target_pairs={{248,0},{0,8},{8,16},{16,24},{24,32},{32,40},{40,48},{48,56},{56,6... | collective-permute-start | bytes 786440 | tf_op jit(solution)/shard_map/while/body/eval_jaxpr/ppermute | solution.py:15
  369.0 9.5 %collective-permute-start = (f32[32,2048]{1,0:T(8,128)S(1)}, f32[32,2048]{1,0:T(8,128)S(1)}, u32[]{:S(2)}, u32[]{:S(2)}) collective-permute-start(f32[32,2048]{1,0:T(8,128)S(1)} %get-tuple-element.195), channel_id=1, source_target_pairs={{248,0},{0,8},{8,16},{16,24},{24,32},{32,40},{40,48},{48,56},{56,6... | collective-permute-start | bytes 786440 | tf_op jit(solution)/shard_map/while/body/eval_jaxpr/ppermute | solution.py:15
  386.1 9.5 %collective-permute-start = (f32[32,2048]{1,0:T(8,128)S(1)}, f32[32,2048]{1,0:T(8,128)S(1)}, u32[]{:S(2)}, u32[]{:S(2)}) collective-permute-start(f32[32,2048]{1,0:T(8,128)S(1)} %get-tuple-element.195), channel_id=1, source_target_pairs={{248,0},{0,8},{8,16},{16,24},{24,32},{32,40},{40,48},{48,56},{56,6... | collective-permute-start | bytes 786440 | tf_op jit(solution)/shard_map/while/body/eval_jaxpr/ppermute | solution.py:15
  403.1 9.5 %collective-permute-start = (f32[32,2048]{1,0:T(8,128)S(1)}, f32[32,2048]{1,0:T(8,128)S(1)}, u32[]{:S(2)}, u32[]{:S(2)}) collective-permute-start(f32[32,2048]{1,0:T(8,128)S(1)} %get-tuple-element.195), channel_id=1, source_target_pairs={{248,0},{0,8},{8,16},{16,24},{24,32},{32,40},{40,48},{48,56},{56,6... | collective-permute-start | bytes 786440 | tf_op jit(solution)/shard_map/while/body/eval_jaxpr/ppermute | solution.py:15
  420.2 9.5 %collective-permute-start = (f32[32,2048]{1,0:T(8,128)S(1)}, f32[32,2048]{1,0:T(8,128)S(1)}, u32[]{:S(2)}, u32[]{:S(2)}) collective-permute-start(f32[32,2048]{1,0:T(8,128)S(1)} %get-tuple-element.195), channel_id=1, source_target_pairs={{248,0},{0,8},{8,16},{16,24},{24,32},{32,40},{40,48},{48,56},{56,6... | collective-permute-start | bytes 786440 | tf_op jit(solution)/shard_map/while/body/eval_jaxpr/ppermute | solution.py:15
  437.3 9.5 %collective-permute-start = (f32[32,2048]{1,0:T(8,128)S(1)}, f32[32,2048]{1,0:T(8,128)S(1)}, u32[]{:S(2)}, u32[]{:S(2)}) collective-permute-start(f32[32,2048]{1,0:T(8,128)S(1)} %get-tuple-element.195), channel_id=1, source_target_pairs={{248,0},{0,8},{8,16},{16,24},{24,32},{32,40},{40,48},{48,56},{56,6... | collective-permute-start | bytes 786440 | tf_op jit(solution)/shard_map/while/body/eval_jaxpr/ppermute | solution.py:15
  454.4 9.5 %collective-permute-start = (f32[32,2048]{1,0:T(8,128)S(1)}, f32[32,2048]{1,0:T(8,128)S(1)}, u32[]{:S(2)}, u32[]{:S(2)}) collective-permute-start(f32[32,2048]{1,0:T(8,128)S(1)} %get-tuple-element.195), channel_id=1, source_target_pairs={{248,0},{0,8},{8,16},{16,24},{24,32},{32,40},{40,48},{48,56},{56,6... | collective-permute-start | bytes 786440 | tf_op jit(solution)/shard_map/while/body/eval_jaxpr/ppermute | solution.py:15
  471.4 9.5 %collective-permute-start = (f32[32,2048]{1,0:T(8,128)S(1)}, f32[32,2048]{1,0:T(8,128)S(1)}, u32[]{:S(2)}, u32[]{:S(2)}) collective-permute-start(f32[32,2048]{1,0:T(8,128)S(1)} %get-tuple-element.195), channel_id=1, source_target_pairs={{248,0},{0,8},{8,16},{16,24},{24,32},{32,40},{40,48},{48,56},{56,6... | collective-permute-start | bytes 786440 | tf_op jit(solution)/shard_map/while/body/eval_jaxpr/ppermute | solution.py:15
  488.5 9.5 %collective-permute-start = (f32[32,2048]{1,0:T(8,128)S(1)}, f32[32,2048]{1,0:T(8,128)S(1)}, u32[]{:S(2)}, u32[]{:S(2)}) collective-permute-start(f32[32,2048]{1,0:T(8,128)S(1)} %get-tuple-element.195), channel_id=1, source_target_pairs={{248,0},{0,8},{8,16},{16,24},{24,32},{32,40},{40,48},{48,56},{56,6... | collective-permute-start | bytes 786440 | tf_op jit(solution)/shard_map/while/body/eval_jaxpr/ppermute | solution.py:15
  505.6 9.5 %collective-permute-start = (f32[32,2048]{1,0:T(8,128)S(1)}, f32[32,2048]{1,0:T(8,128)S(1)}, u32[]{:S(2)}, u32[]{:S(2)}) collective-permute-start(f32[32,2048]{1,0:T(8,128)S(1)} %get-tuple-element.195), channel_id=1, source_target_pairs={{248,0},{0,8},{8,16},{16,24},{24,32},{32,40},{40,48},{48,56},{56,6... | collective-permute-start | bytes 786440 | tf_op jit(solution)/shard_map/while/body/eval_jaxpr/ppermute | solution.py:15
  522.7 9.5 %collective-permute-start = (f32[32,2048]{1,0:T(8,128)S(1)}, f32[32,2048]{1,0:T(8,128)S(1)}, u32[]{:S(2)}, u32[]{:S(2)}) collective-permute-start(f32[32,2048]{1,0:T(8,128)S(1)} %get-tuple-element.195), channel_id=1, source_target_pairs={{248,0},{0,8},{8,16},{16,24},{24,32},{32,40},{40,48},{48,56},{56,6... | collective-permute-start | bytes 786440 | tf_op jit(solution)/shard_map/while/body/eval_jaxpr/ppermute | solution.py:15
  539.8 9.5 %collective-permute-start = (f32[32,2048]{1,0:T(8,128)S(1)}, f32[32,2048]{1,0:T(8,128)S(1)}, u32[]{:S(2)}, u32[]{:S(2)}) collective-permute-start(f32[32,2048]{1,0:T(8,128)S(1)} %get-tuple-element.195), channel_id=1, source_target_pairs={{248,0},{0,8},{8,16},{16,24},{24,32},{32,40},{40,48},{48,56},{56,6... | collective-permute-start | bytes 786440 | tf_op jit(solution)/shard_map/while/body/eval_jaxpr/ppermute | solution.py:15
  (4 other events, 1599.3 us)
Sparse Core Ops, SparseCore 0:
  557.7 31.8 reduce-scatter.1
where the time goes:
time: 600 us; the launch traced here: 598 us
  waiting for transfers between devices  325 us (54%)
  matrix products  242 us (40%)
  between operations  13.4 us (2%)
  local copies, waits for them, and re-layouts  11.7 us (2%)
    ppermute x31, waiting for transfers between devices, passed_along(): return lax.ppermute(block, axis, route)  293 us
    dot_general x32, matrix products, contract(): lax.dot_general(columns, wmat, (((0,), (0,)), ((), ())), precision=lax.Pr...  242 us
    reduce_scatter x1, waiting for transfers between devices, shards(): summed = lax.psum_scatter(carried, 'rep', scatter_dimension=1, tiled=True)  31.6 us
  transfers between devices with their start and end apart: 32, of which 32 were waited for; matrix products, arithmetic and copies ran while one was open for 0% of the time, Pallas kernels for 0%

commit v1 on v0

v1 whole, which is shorter than its diff:
```python
import jax
import jax.numpy as jnp
from jax import lax
from jax.experimental import pallas as pl
from jax.experimental.pallas import tpu as pltpu
from jax.sharding import PartitionSpec as P

MESH = pl.DeviceIdType.MESH
F32 = jnp.float32
BF16 = jnp.bfloat16

NX, NY, NZ = 4, 4, 8
ROWS, COLS = 32, 256
UNITS = 8
LANES = 128
TOP = 24


def copy_to(src, dst, sems, at, device):
    return pltpu.make_async_remote_copy(
        src_ref=src,
        dst_ref=dst,
        send_sem=sems[0].at[at],
        recv_sem=sems[1].at[at],
        device_id=device,
        device_id_type=MESH,
    )


def kernel(
    t_hbm, w_hbm, out_ref,
    t_raw, w_raw, tcat, wcat, own, sent, got, hx, hy, hz,
    rx1, rx2, ry1, ry2, rzh, rz, rx3, rx4, ry3, ry4, rz5, rz6, rf, rz7,
    load_t, load_w,
    c_s, c_r, x1_s, x1_r, x2_s, x2_r, y1_s, y1_r, y2_s, y2_r, zh_s, zh_r, z_s, z_r,
    x3_s, x3_r, x4_s, x4_r, y3_s, y3_r, y4_s, y4_r, z5_s, z5_r, z6_s, z6_r,
    f_s, f_r, z7_s, z7_r,
):
    depth = t_hbm.shape[0]
    blk, rep = lax.axis_index("blk"), lax.axis_index("rep")
    core, z, y_hi = blk % 2, (blk // 2) % NZ, blk // (2 * NZ)
    x, y_lo = rep // 2, rep % 2
    y = 2 * y_hi + y_lo

    def along_x(d):
        return (blk, ((x + d + NX) % NX) * 2 + y_lo)

    def along_y(d):
        there = (y + d + NY) % NY
        return ((there // 2) * 2 * NZ + z * 2 + core, x * 2 + there % 2)

    def along_z(d):
        return (y_hi * 2 * NZ + ((z + d + NZ) % NZ) * 2 + core, rep)

    other_core = (blk + 1 - 2 * core, rep)
    z_at = lambda d: (z + d + NZ) % NZ
    yh_right = ((y + 1) % NY) // 2
    yh_left = ((y + 3) % NY) // 2

    barrier = pltpu.get_barrier_semaphore()
    friends = [other_core, along_x(1), along_x(-1), along_y(1), along_y(-1), along_y(2)]
    friends += [along_z(d) for d in range(1, NZ)]
    for friend in friends:
        pl.semaphore_signal(barrier, inc=1, device_id=friend, device_id_type=MESH)

    t_loads = [
        pltpu.make_async_copy(t_hbm.at[:, pl.ds(LANES * j, LANES)], t_raw.at[j], load_t.at[j])
        for j in range(8)
    ]
    part = w_hbm.shape[0] // 8
    w_loads = [
        pltpu.make_async_copy(
            w_hbm.at[pl.ds(part * j, part)], w_raw.at[pl.ds(part * j, part)], load_w.at[j]
        )
        for j in range(8)
    ]
    for load in t_loads + w_loads:
        load.start()

    step = 256

    def split(value):
        high = value.astype(BF16)
        return high, (value - high.astype(F32)).astype(BF16)

    def turn(j, _):
        pltpu.make_async_copy(t_hbm.at[:, pl.ds(0, LANES)], t_raw.at[j], load_t.at[j]).wait()
        for k in range(0, depth, step):
            high, low = split(t_raw[j, k : k + step, :].T)
            for m in range(4):
                rows = pl.ds(pl.multiple_of(64 * j + 32 * (m // 2), 32), 32)
                these = slice(32 * m, 32 * m + 32)
                tcat[m % 2, rows, k : k + step] = high[these]
                tcat[m % 2, rows, depth + k : depth + k + step] = low[these]
                tcat[m % 2, rows, 2 * depth + k : 2 * depth + k + step] = high[these]
        return 0

    lax.fori_loop(0, 8, turn, 0)
    for load in w_loads:
        load.wait()
    pl.semaphore_wait(barrier, len(friends))

    def take_columns(u):
        h, i = u // 4, u % 4
        ahead = (i // 2) * 3 * (3 - i) + (1 - i // 2) * (2 - i)
        a = (x + ahead) % NX
        b = (y_lo + h) % 2
        for c in range(2):
            for k in range(0, depth, step):
                start = k * 16 + (2 * b + c) * 4 + a
                high, low = split(w_raw[pl.ds(start, step, stride=16), :])
                lanes = slice(c * LANES, (c + 1) * LANES)
                wcat[k : k + step, lanes] = high
                wcat[depth + k : depth + k + step, lanes] = high
                wcat[2 * depth + k : 2 * depth + k + step, lanes] = low

    def product(which):
        value = jnp.dot(tcat[which], wcat[...], preferred_element_type=F32)
        return value.reshape(16, ROWS, COLS)

    def to_core(u):
        return copy_to(sent.at[u], got.at[u], (c_s, c_r), u, other_core)

    def x1(h, d):
        return copy_to(hx.at[h, 0, d], rx1.at[h, d], (x1_s, x1_r), (h, d), along_x(1 - 2 * d))

    def x2(h, d, half):
        return copy_to(
            hx.at[h, 1 + d, half], rx2.at[h, d, half], (x2_s, x2_r), (h, d, half), along_x(1 - 2 * d)
        )

    def x_final(h):
        for half in range(2):
            for d in range(2):
                x2(h, d, half).wait_recv()
            hx[h, 3, half] = hx[h, 3, half] + rx2[h, 0, half] + rx2[h, 1, half]

    def y1(i, d):
        return copy_to(
            hy.at[0, i, 1 - y_hi, pl.ds(4 * d, 4)], ry1.at[i, d], (y1_s, y1_r), (i, d), along_y(1 - 2 * d)
        )

    def y2(i, d):
        return copy_to(
            hy.at[1, i, (yh_right, yh_left)[d]], ry2.at[i, d], (y2_s, y2_r), (i, d), along_y(1 - 2 * d)
        )

    def y_next(i, d):
        yh, these = (yh_right, yh_left)[d], pl.ds(4 * d, 4)
        y1(i, d).wait_recv()
        hy[1, i, yh, these] = hy[1, i, yh, these] + ry1[i, d]
        y2(i, d).start()

    def zh(q, d):
        return copy_to(
            hz.at[q // 2, q % 2, :, d, z_at(4)], rzh.at[q, d], (zh_s, zh_r), (q, d), along_z(1 - 2 * d)
        )

    def zf(q, d, s):
        chunk = z_at((1 - 2 * d) * (3 - s))
        return copy_to(
            hz.at[q // 2, q % 2, :, :, chunk], rz.at[q, d, s], (z_s, z_r), (q, d, s), along_z(1 - 2 * d)
        )

    def z_second(q):
        for d in range(2):
            chunk = z_at((1 - 2 * d) * 3)
            zh(q, d).wait_recv()
            hz[q // 2, q % 2, :, d, chunk] = hz[q // 2, q % 2, :, d, chunk] + rzh[q, d]
            zf(q, d, 0).start()

    def z_later(q, s):
        for d in range(2):
            chunk = z_at((1 - 2 * d) * (3 - s))
            zf(q, d, s - 1).wait_recv()
            hz[q // 2, q % 2, :, :, chunk] = hz[q // 2, q % 2, :, :, chunk] + rz[q, d, s - 1]
            zf(q, d, s).start()

    def z_final(q):
        for d in range(2):
            zf(q, d, 2).wait_recv()
        h, g = q // 2, q % 2
        hz[h, g, :, :, z] = hz[h, g, :, :, z] + rz[q, 0, 2] + rz[q, 1, 2]

    def z_steps(u):
        even = u % 2 == 0

        @pl.when(jnp.logical_not(even) & (u < 8))
        def _():
            for d in range(2):
                zh(u // 2, d).start()

        @pl.when(even & (u >= 2) & (u < 10))
        def _():
            z_second(u // 2 - 1)

        @pl.when(jnp.logical_not(even) & (u >= 3) & (u < 11))
        def _():
            z_later((u - 3) // 2, 1)

        @pl.when(even & (u >= 4) & (u < 12))
        def _():
            z_later(u // 2 - 2, 2)

        @pl.when(jnp.logical_not(even) & (u >= 5))
        def _():
            z_final((u - 5) // 2)

    def x3(d):
        return copy_to(hx.at[0, 3, 1 - y_hi, pl.ds(4 * d, 4)], rx3.at[d], (x3_s, x3_r), d, along_y(1 - 2 * d))

    def x4(d):
        return copy_to(hx.at[1, 3, (yh_right, yh_left)[d]], rx4.at[d], (x4_s, x4_r), d, along_y(1 - 2 * d))

    def y3(d):
        return copy_to(hy.at[0, 0, y_hi, pl.ds(4 * d, 4)], ry3.at[d], (y3_s, y3_r), d, along_x(1 - 2 * d))

    def y4(d):
        return copy_to(hy.at[0, 1 + d, y_hi], ry4.at[d], (y4_s, y4_r), d, along_x(1 - 2 * d))

    def z5(d):
        return copy_to(hz.at[d, 0, 0, :, z], rz5.at[d], (z5_s, z5_r), d, along_x(1 - 2 * d))

    def z6(d):
        return copy_to(hz.at[:, d, 1 - d, :, z], rz6.at[d], (z6_s, z6_r), d, along_x(1 - 2 * d))

    def last(p, d):
        src = hx.at[0, 3, y_hi, z_at(d)] if p == 0 else hy.at[0, 3, y_hi, z_at(d)]
        return copy_to(src, rf.at[p, d - 1], (f_s, f_r), (p, d - 1), along_z(d))

    def z7(d):
        src = hz.at[1, 1, 1, (yh_right, yh_left)[d], z] if d < 2 else hz.at[0, 1, 1, 1 - y_hi, z]
        return copy_to(src, rz7.at[d], (z7_s, z7_r), d, along_y((1, -1, 2)[d]))

    def events(u):
        h, i = u // 4, u % 4
        to_core(u).wait_recv()
        for half in range(2):
            rows = pl.ds(8 * half, 8)
            hx[h, i, half] = own[u % 2, rows, :TOP, :LANES] + got[u, rows, :TOP, :LANES]
            hy[h, i, half] = own[u % 2, rows, :TOP, LANES:] + got[u, rows, :TOP, LANES:]
            hz[h, i // 2, i % 2, half] = own[u % 2, rows, TOP:, :] + got[u, rows, TOP:, :]

        @pl.when(i == 0)
        def _():
            for d in range(2):
                x1(h, d).start()

        @pl.when(i == 1)
        def _():
            x2(h, 0, 1).start()

        @pl.when(i == 2)
        def _():
            x2(h, 1, 0).start()
            x1(h, 0).wait_recv()
            hx[h, 1, 0] = hx[h, 1, 0] + rx1[h, 0]
            x2(h, 0, 0).start()

        @pl.when(i == 3)
        def _():
            x1(h, 1).wait_recv()
            hx[h, 2, 1] = hx[h, 2, 1] + rx1[h, 1]
            x2(h, 1, 1).start()

        @pl.when(h == 0)
        def _():
            for d in range(2):
                y1(i, d).start()

        @pl.when(h == 1)
        def _():
            for d in range(2):
                y_next(i, d)

        z_steps(u)

        @pl.when(u == 7)
        def _():
            x_final(0)
            for d in range(2):
                x3(d).start()

    def turn_units(v, _):
        @pl.when(v < UNITS)
        def _():
            take_columns(v)
            sent[v] = product(1 - core)
            to_core(v).start()

        @pl.when(v > 0)
        def _():
            events(v - 1)

        @pl.when(v < UNITS)
        def _():
            own[v % 2] = product(core)

        return 0

    lax.fori_loop(0, UNITS + 1, turn_units, 0)
    lax.fori_loop(UNITS, 12, lambda u, _: (z_steps(u), 0)[1], 0)

    for d in range(2):
        z5(d).start()
    x_final(1)
    for d in range(2):
        yh, these = (yh_right, yh_left)[d], pl.ds(4 * d, 4)
        x3(d).wait_recv()
        hx[1, 3, yh, these] = hx[1, 3, yh, these] + rx3[d]
        x4(d).start()
    for i in range(4):
        for d in range(2):
            y2(i, d).wait_recv()
        hy[0, i, y_hi] = hy[0, i, y_hi] + ry2[i, 0] + ry2[i, 1]
        if i == 0:
            for d in range(2):
                y3(d).start()
    for d in range(2):
        z5(d).wait_recv()
        hz[d, d, 1 - d, :, z] = hz[d, d, 1 - d, :, z] + rz5[d]
        z6(d).start()
    for d in range(2):
        these = pl.ds(4 * d, 4)
        y3(d).wait_recv()
        hy[0, 1 + d, y_hi, these] = hy[0, 1 + d, y_hi, these] + ry3[d]
        y4(d).start()
    for d in range(2):
        x4(d).wait_recv()
    hx[0, 3, y_hi] = hx[0, 3, y_hi] + rx4[0] + rx4[1]
    for d in range(1, NZ):
        last(0, d).start()
    for d in range(2):
        z6(d).wait_recv()
    hz[:, 1, 1, :, z] = hz[:, 1, 1, :, z] + rz6[0] + rz6[1]
    for d in range(3):
        z7(d).start()
    for d in range(2):
        y4(d).wait_recv()
    hy[0, 3, y_hi] = hy[0, 3, y_hi] + ry4[0] + ry4[1]
    for d in range(1, NZ):
        last(1, d).start()

    for p, mine in ((0, hx), (1, hy)):
        total = mine[0, 3, y_hi, z]
        for d in range(1, NZ):
            last(p, d).wait_recv()
            total = total + rf[p, d - 1]
        out_ref[:TOP, p * LANES : (p + 1) * LANES] = total
    total = hz[0, 1, 1, y_hi, z]
    for d in range(3):
        z7(d).wait_recv()
        total = total + rz7[d]
    out_ref[TOP:, :] = total

    def sent_all(u, _):
        to_core(u).wait_send()
        return 0

    def sent_groups(q, _):
        for d in range(2):
            y1(q, d).wait_send()
            y2(q, d).wait_send()
            zh(q, d).wait_send()
            for s in range(3):
                zf(q, d, s).wait_send()
        return 0

    lax.fori_loop(0, UNITS, sent_all, 0)
    lax.fori_loop(0, 4, sent_groups, 0)
    for d in range(2):
        for h in range(2):
            x1(h, d).wait_send()
            for half in range(2):
                x2(h, d, half).wait_send()
        for sending in (x3, x4, y3, y4, z5, z6):
            sending(d).wait_send()
    for d in range(1, NZ):
        for p in range(2):
            last(p, d).wait_send()
    for d in range(3):
        z7(d).wait_send()


def reduced(t, w):
    depth = t.shape[0]
    buffers = [
        ((8, depth, LANES), F32),
        (w.shape, F32),
        ((2, 16 * ROWS, 3 * depth), BF16),
        ((3 * depth, COLS), BF16),
        ((2, 16, ROWS, COLS), F32),
        ((UNITS, 16, ROWS, COLS), F32),
        ((UNITS, 16, ROWS, COLS), F32),
        ((2, 4, 2, 8, TOP, LANES), F32),
        ((2, 4, 2, 8, TOP, LANES), F32),
        ((2, 2, 2, 2, 8, ROWS - TOP, COLS), F32),
        ((2, 2, 8, TOP, LANES), F32),
        ((2, 2, 2, 8, TOP, LANES), F32),
        ((4, 2, 4, TOP, LANES), F32),
        ((4, 2, 8, TOP, LANES), F32),
        ((4, 2, 2, ROWS - TOP, COLS), F32),
        ((4, 2, 3, 2, 2, ROWS - TOP, COLS), F32),
        ((2, 4, TOP, LANES), F32),
        ((2, 8, TOP, LANES), F32),
        ((2, 4, TOP, LANES), F32),
        ((2, 8, TOP, LANES), F32),
        ((2, 2, ROWS - TOP, COLS), F32),
        ((2, 2, 2, ROWS - TOP, COLS), F32),
        ((2, 7, TOP, LANES), F32),
        ((3, ROWS - TOP, COLS), F32),
    ]
    pairs = [(8,), (2, 2), (2, 2, 2), (4, 2), (4, 2), (4, 2), (4, 2, 3)] + [(2,)] * 6 + [(2, 7), (3,)]
    sems = [pltpu.SemaphoreType.DMA((8,))] * 2
    for shape in pairs:
        sems += [pltpu.SemaphoreType.DMA(shape)] * 2
    return pl.pallas_call(
        kernel,
        out_shape=jax.ShapeDtypeStruct((ROWS, COLS), F32),
        in_specs=[pl.BlockSpec(memory_space=pl.ANY)] * 2,
        out_specs=pl.BlockSpec(memory_space=pltpu.VMEM),
        scratch_shapes=[pltpu.VMEM(shape, kind) for shape, kind in buffers] + sems,
        compiler_params=pltpu.CompilerParams(
            collective_id=0, has_side_effects=True, vmem_limit_bytes=56 * 2**20
        ),
    )(t, w)


def shards(amplitudes, integrals, occ_energy, virt_energy, outer_energy):
    depth = amplitudes.shape[0] * amplitudes.shape[1]
    t = amplitudes.reshape(depth, amplitudes.shape[2])
    w = integrals.reshape(depth, 4, 4, LANES).transpose(0, 2, 1, 3).reshape(depth * 16, LANES)
    summed = reduced(t, w)
    blk, rep = lax.axis_index("blk"), lax.axis_index("rep")
    first = lax.dynamic_slice_in_dim(occ_energy, blk // 2, 1, 0)
    second = lax.dynamic_slice_in_dim(occ_energy, (blk % 2) * ROWS, ROWS, 0)
    outer = lax.dynamic_slice_in_dim(outer_energy, rep // 2, 1, 0)
    virt = lax.dynamic_slice_in_dim(virt_energy, (rep % 2) * COLS, COLS, 0)
    return summed / ((outer + virt)[None, :] - (first + second)[:, None])


def solution(mesh):
    placed = (P("blk", "rep", None), P("blk", "rep", None, None), P(), P(), P())
    return jax.shard_map(
        shards, mesh=mesh, in_specs=placed, out_specs=P("blk", "rep"), check_vma=False
    )
```

time: 600 us -> 68.8 us (0.11)
  waiting for transfers between devices: 325 us -> 0 us
  matrix products: 242 us -> 0 us
  Pallas kernels: 0 us -> 61.6 us
  between operations: 13.4 us -> 0.01 us
  local copies, waits for them, and re-layouts: 11.7 us -> 2.47 us
    ppermute x31 -> x0, waiting for transfers between devices: 293 us -> none  [passed_along(): return lax.ppermute(block, axis, route)]
    dot_general x32 -> x0, matrix products: 242 us -> none  [contract(): lax.dot_general(columns, wmat, (((0,), (0,)), ((), ())), precision=lax.Pr...]
    pallas_call x0 -> x1, Pallas kernels: none -> 61.6 us  [reduced(): pl.pallas_call(kernel, out_shape=jax.ShapeDtypeStruct((ROWS, COLS), F32),...]
    reduce_scatter x1 -> x0, waiting for transfers between devices: 31.6 us -> none  [shards(): summed = lax.psum_scatter(carried, 'rep', scatter_dimension=1, tiled=True)]
    unnamed x10 -> x0, local copies, waits for them, and re-layouts: 11.4 us -> none
  transfers between devices with their start and end apart: 32 -> 0, of which waited for: 32 -> 0; matrix products, arithmetic and copies ran while one was open for 0% -> 0% of each run, Pallas kernels for 0% -> 0%
where the time goes in v1:
time: 68.8 us; the launch traced here: 68.3 us
  Pallas kernels  61.6 us (90%)
  other arithmetic  4.23 us (6%)
  local copies, waits for them, and re-layouts  2.47 us (4%)
    pallas_call x1, Pallas kernels, reduced(): pl.pallas_call(kernel, out_shape=jax.ShapeDtypeStruct((ROWS, COLS), F32),...  61.6 us
    add x2, other arithmetic, shards(): return summed / ((outer + virt)[None, :] - (first + second)[:, None])  2.78 us
    div x1, other arithmetic, shards(): return summed / ((outer + virt)[None, :] - (first + second)[:, None])  1.45 us

profile of v1, /device:TPU:2, one launch (start us, length us, event | category | flops | bytes accessed | tf_op | source)
XLA Modules:
  0.0 68.3 jit_solution(17943652316115744588)
XLA Ops:
  0.0 1.2 %dynamic_slice.14 = f32[1]{0:T(128)} dynamic-slice(f32[64]{0:T(128)} %param.7, s32[]{:T(128)S(6)} %select_n.35), dynamic_slice_sizes={1} | dynamic-slice | bytes 12 | tf_op jit(solution)/shard_map/dynamic_slice | solution.py:435
  1.2 1.4 %dynamic-slice_add_fusion.1 = f32[32]{0:T(128)S(1)} fusion(f32[64]{0:T(128)} %param.7, s32[]{:T(128)S(6)} %select_n.37, f32[]{:T(128)} %bitcast.5), kind=kLoop, calls=%fused_computation.2 | loop fusion | flops 32 | bytes 264 | tf_op jit(solution)/shard_map/add | solution.py:439
  2.6 1.2 %dynamic_slice.12 = f32[1]{0:T(128)} dynamic-slice(f32[4]{0:T(128)} %param.9, s32[]{:T(128)S(6)} %select_n.31), dynamic_slice_sizes={1} | dynamic-slice | bytes 12 | tf_op jit(solution)/shard_map/dynamic_slice | solution.py:437
  3.9 1.4 %dynamic-slice_add_fusion = f32[256]{0:T(256)S(1)} fusion(f32[512]{0:T(512)} %param.8, s32[]{:T(128)S(6)} %select_n.33, f32[]{:T(128)} %bitcast.4), kind=kLoop, calls=%fused_computation.1 | loop fusion | flops 256 | bytes 2056 | tf_op jit(solution)/shard_map/add | solution.py:439
  5.3 61.6 %shard_map.55 = f32[32,256]{1,0:T(8,128)} custom-call(f32[1024,1024]{1,0:T(8,128)} %bitcast.9, f32[16384,128]{1,0:T(8,128)} %bitcast.8), custom_call_target="tpu_custom_call" | custom-call | tf_op jit(solution)/shard_map/pallas_call | solution.py:417
  66.8 1.5 %subtract_divide_fusion = f32[32,256]{1,0:T(8,128)} fusion(f32[32,256]{1,0:T(8,128)} %shard_map.55, f32[32]{0:T(128)S(1)} %dynamic-slice_add_fusion.1, f32[256]{0:T(256)S(1)} %dynamic-slice_add_fusion), kind=kLoop, calls=%fused_computation | loop fusion | flops 16384 | bytes 66688 | tf_op jit(solution)/shard_map/div | solution.py:439

commit v2 on v0

v2 whole, which is shorter than its diff:
```python
import jax
import jax.numpy as jnp
from jax import lax
from jax.experimental import pallas as pl
from jax.experimental.pallas import tpu as pltpu
from jax.sharding import PartitionSpec as P

MESH = pl.DeviceIdType.MESH
F32 = jnp.float32
BF16 = jnp.bfloat16

NX, NY, NZ = 4, 4, 8
ROWS, COLS = 32, 256
UNITS = 8
LANES = 128
TOP = 24
LOW = ROWS - TOP

BUFFERS = {
    "t_raw": ((8, 1024, LANES), F32),
    "w_raw": ((16384, LANES), F32),
    "tcat": ((2, 2, 256, 3072), BF16),
    "wcat": ((3072, 2 * COLS), BF16),
    "own": ((2, 2, 8, ROWS, COLS), F32),
    "sent": ((UNITS, 2, 8, ROWS, COLS), F32),
    "got": ((UNITS, 2, 8, ROWS, COLS), F32),
    "hx": ((2, 4, 2, 2, 4, TOP, LANES), F32),
    "hy": ((2, 4, 2, 2, 4, TOP, LANES), F32),
    "hz": ((2, 4, 2, 2, 4, LOW, COLS), F32),
    "rx1": ((2, 2, 2, 4, TOP, LANES), F32),
    "rx2": ((2, 2, 2, 2, 4, TOP, LANES), F32),
    "ry1": ((2, 3, 2, 2, TOP, LANES), F32),
    "ryd": ((2, 4, TOP, LANES), F32),
    "ry2": ((2, 4, 2, 4, TOP, LANES), F32),
    "rzh": ((4, 2, 2, LOW, COLS), F32),
    "rz3": ((4, 2, 2, 2, LOW, COLS), F32),
    "rz2": ((4, 2, 2, 2, LOW, COLS), F32),
    "rz1": ((4, 2, 2, 2, LOW, COLS), F32),
    "rx3": ((2, 2, 2, TOP, LANES), F32),
    "rx4": ((2, 2, 4, TOP, LANES), F32),
    "ry3": ((2, 2, 2, TOP, LANES), F32),
    "ry4": ((2, 2, 4, TOP, LANES), F32),
    "rz5": ((3, 2, 2, LOW, COLS), F32),
    "rf": ((2, 7, TOP, LANES), F32),
    "rz7": ((3, LOW, COLS), F32),
    "virt": ((4, LANES), F32),
    "den": ((2, ROWS, LANES), F32),
}
SENDS = {
    "c": (8,), "x1": (2, 2), "x2": (2, 2, 2), "y1": (2, 3, 2), "yd": (2,), "y2": (2, 4, 2),
    "zh": (4, 2), "z3": (4, 2), "z2": (4, 2), "z1": (4, 2), "x3": (2, 2), "x4": (2, 2),
    "y3": (2, 2), "y4": (2, 2), "z5": (3,), "f": (2, 7), "z7": (3,),
}


def kernel(t_hbm, w_hbm, occ_hbm, virt_hbm, outer_hbm, out_ref, *refs):
    names = list(BUFFERS)
    (t_raw, w_raw, tcat, wcat, own, sent, got, hx, hy, hz, rx1, rx2, ry1, ryd, ry2, rzh, rz3, rz2, rz1,
     rx3, rx4, ry3, ry4, rz5, rf, rz7, virt, den) = refs[: len(names)]
    occ, outer, load_t, load_w, load_e = refs[len(names) : len(names) + 5]
    left = refs[len(names) + 5 :]
    sems = {name: (left[2 * n], left[2 * n + 1]) for n, name in enumerate(SENDS)}

    depth = t_hbm.shape[0]
    blk, rep = lax.axis_index("blk"), lax.axis_index("rep")
    core, z, y_hi = blk % 2, (blk // 2) % NZ, blk // (2 * NZ)
    x, y_lo = rep // 2, rep % 2
    y = 2 * y_hi + y_lo
    beside = (y_lo, 1 - y_lo)
    way = (1, -1)

    def along_x(d):
        return (blk, ((x + d + NX) % NX) * 2 + y_lo)

    def along_y(d):
        there = (y + d + NY) % NY
        return ((there // 2) * 2 * NZ + z * 2 + core, x * 2 + there % 2)

    def along_z(d):
        return (y_hi * 2 * NZ + ((z + d + NZ) % NZ) * 2 + core, rep)

    other_core = (blk + 1 - 2 * core, rep)

    def put(src, dst, name, at, device):
        return pltpu.make_async_remote_copy(
            src_ref=src,
            dst_ref=dst,
            send_sem=sems[name][0].at[at],
            recv_sem=sems[name][1].at[at],
            device_id=device,
            device_id_type=MESH,
        )

    barrier = pltpu.get_barrier_semaphore()
    friends = [other_core, along_x(1), along_x(-1), along_x(2), along_y(1), along_y(-1), along_y(2)]
    friends += [along_z(d) for d in range(1, NZ)]
    for friend in friends:
        pl.semaphore_signal(barrier, inc=1, device_id=friend, device_id_type=MESH)

    small = [
        pltpu.make_async_copy(occ_hbm, occ, load_e.at[0]),
        pltpu.make_async_copy(virt_hbm, virt, load_e.at[1]),
        pltpu.make_async_copy(outer_hbm, outer, load_e.at[2]),
    ]
    for j in range(8):
        pltpu.make_async_copy(t_hbm.at[:, pl.ds(LANES * j, LANES)], t_raw.at[j], load_t.at[j]).start()
    for load in small:
        load.start()
    part = w_hbm.shape[0] // 8

    def load_columns(j):
        these = pl.ds(pl.multiple_of(part * j, part), part)
        return pltpu.make_async_copy(w_hbm.at[these], w_raw.at[these], load_w.at[j])

    step = 256

    def split(value):
        high = value.astype(BF16)
        return high, (value - high.astype(F32)).astype(BF16)

    def turn(j, _):
        pltpu.make_async_copy(t_hbm.at[:, pl.ds(0, LANES)], t_raw.at[j], load_t.at[j]).wait()
        load_columns(j).start()
        g = (j // 4 + y_hi) % 2
        for k in range(0, depth, step):
            high, low = split(t_raw[j, k : k + step, :].T)
            for m in range(4):
                slot = ((2 * j + m // 2) % NZ - z - 2 + 2 * NZ) % NZ
                rows = pl.ds(pl.multiple_of(g * 128 + (slot % 4) * 32, 32), 32)
                these = slice(32 * m, 32 * m + 32)
                tcat[m % 2, slot // 4, rows, k : k + step] = high[these]
                tcat[m % 2, slot // 4, rows, depth + k : depth + k + step] = low[these]
                tcat[m % 2, slot // 4, rows, 2 * depth + k : 2 * depth + k + step] = high[these]
        return 0

    lax.fori_loop(0, 8, turn, 0)

    for load in small:
        load.wait()
    at_row = lax.broadcasted_iota(jnp.int32, (ROWS, LANES), 0)
    pair = jnp.zeros((ROWS, LANES), F32)
    for r in range(ROWS):
        pair = jnp.where(at_row == r, occ[blk // 2] + occ[(blk % 2) * ROWS + r], pair)
    for c in range(2):
        den[c] = (outer[x] + virt[pl.ds(2 * y_lo + c, 1), :]) - pair

    for j in range(8):
        load_columns(j).wait()

    def piece(v, p):
        last = v // 3
        mid = (v + 1) // 2 - 2 * last
        one = mid - (v // 2 - last)
        return mid * (1 + p) + 3 * last, p + one * (1 - 2 * p)

    def take_columns(u):
        for p in range(2):
            i, h = piece(u % 4, p)
            ahead = (i // 2) * 3 * (3 - i) + (1 - i // 2) * (2 - i)
            a = (x + ahead) % NX
            b = (y_lo + h) % 2
            for c in range(2):
                for k in range(0, depth, step):
                    start = k * 16 + (2 * b + c) * 4 + a
                    high, low = split(w_raw[pl.ds(start, step, stride=16), :])
                    lanes = slice(p * COLS + c * LANES, p * COLS + (c + 1) * LANES)
                    wcat[k : k + step, lanes] = high
                    wcat[depth + k : depth + k + step, lanes] = high
                    wcat[2 * depth + k : 2 * depth + k + step, lanes] = low

    def product(which, half, dst, at):
        value = jnp.dot(tcat[which, half], wcat[...], preferred_element_type=F32)
        for p in range(2):
            dst[at, p] = value[:, p * COLS : (p + 1) * COLS].reshape(8, ROWS, COLS)

    def to_core(u):
        return put(sent.at[u], got.at[u], "c", u, other_core)

    def x1(s, d):
        return put(hx.at[s, 0, d], rx1.at[s, d], "x1", (s, d), along_x(way[d]))

    def x2(s, d, h):
        return put(hx.at[s, 1 + d, h], rx2.at[s, d, h], "x2", (s, d, h), along_x(way[d]))

    def x_final(s):
        for h in range(2):
            for d in range(2):
                x2(s, d, h).wait_recv()
            hx[s, 3, h] = hx[s, 3, h] + rx2[s, 0, h] + rx2[s, 1, h]

    def x3(s, d):
        return put(hx.at[s, 3, 0, 1, pl.ds(2 * d, 2)], rx3.at[s, d], "x3", (s, d), along_y(way[d]))

    def x4(s, d):
        return put(hx.at[s, 3, 1, beside[d]], rx4.at[s, d], "x4", (s, d), along_y(way[d]))

    def x_on(s):
        for d in range(2):
            these = pl.ds(2 * d, 2)
            x3(s, d).wait_recv()
            hx[s, 3, 1, beside[d], these] = hx[s, 3, 1, beside[d], these] + rx3[s, d]
            x4(s, d).start()

    def y1(s, i, d):
        return put(hy.at[s, i, 0, 1, pl.ds(2 * d, 2)], ry1.at[s, i, d], "y1", (s, i, d), along_y(way[d]))

    def yd(s):
        return put(hy.at[s, 3, 0, 1], ryd.at[s], "yd", s, along_y(2))

    def y2(s, i, d):
        return put(hy.at[s, i, 1, beside[d]], ry2.at[s, i, d], "y2", (s, i, d), along_y(way[d]))

    def y_start(s, i):
        for d in range(2):
            y1(s, i, d).start()

    def y_next(s, i):
        for d in range(2):
            these = pl.ds(2 * d, 2)
            y1(s, i, d).wait_recv()
            hy[s, i, 1, beside[d], these] = hy[s, i, 1, beside[d], these] + ry1[s, i, d]
            y2(s, i, d).start()

    def y_final(s, i):
        for d in range(2):
            y2(s, i, d).wait_recv()
        total = hy[s, i, 0, 0] + ry2[s, i, 0] + ry2[s, i, 1]
        if i == 3:
            yd(s).wait_recv()
            total = total + ryd[s]
        hy[s, i, 0, 0] = total

    def y3(s, d):
        return put(hy.at[s, 0, 0, 0, pl.ds(2 * d, 2)], ry3.at[s, d], "y3", (s, d), along_x(way[d]))

    def y4(s, d):
        return put(hy.at[s, 1 + d, 0, 0], ry4.at[s, d], "y4", (s, d), along_x(way[d]))

    def y_on(s):
        for d in range(2):
            these = pl.ds(2 * d, 2)
            y3(s, d).wait_recv()
            hy[s, 1 + d, 0, 0, these] = hy[s, 1 + d, 0, 0, these] + ry3[s, d]
            y4(s, d).start()

    def zh(v, d):
        return put(hz.at[0, v, :, d, 2], rzh.at[v, d], "zh", (v, d), along_z(way[d]))

    def z3(v, d):
        return put(hz.at[0, v, :, :, 1 + 2 * d], rz3.at[v, d], "z3", (v, d), along_z(way[d]))

    def z2(v, d):
        return put(hz.at[d, v, :, :, 0], rz2.at[v, d], "z2", (v, d), along_z(2 * way[d]))

    def z1(v, d):
        return put(hz.at[1, v, :, :, 3 - 2 * d], rz1.at[v, d], "z1", (v, d), along_z(way[d]))

    def z_second(v):
        for d in range(2):
            zh(v, d).wait_recv()
            hz[0, v, :, d, 1 + 2 * d] = hz[0, v, :, d, 1 + 2 * d] + rzh[v, d]
            z3(v, d).start()

    def z_third(v, d):
        z3(v, d).wait_recv()
        hz[d, v, :, :, 0] = hz[d, v, :, :, 0] + rz3[v, d]
        z2(v, d).start()

    def z_final(v):
        for d in range(2):
            z2(v, d).wait_recv()
            z1(v, d).wait_recv()
        hz[1, v, :, :, 2] = (
            hz[1, v, :, :, 2] + (rz2[v, 0] + rz2[v, 1]) + (rz1[v, 0] + rz1[v, 1])
        )

    def z5(n):
        src = hz.at[1, 0, :, :, 2] if n == 0 else hz.at[1, 1:3, n - 1, :, 2]
        return put(src, rz5.at[n], "z5", n, along_x((2, 1, -1)[n]))

    def z7(n):
        src = hz.at[1, 3, 1, beside[n], 2] if n < 2 else hz.at[1, 3, 0, 1, 2]
        return put(src, rz7.at[n], "z7", n, along_y((1, -1, 2)[n]))

    def last(p, d):
        s, k = ((d - 2) % NZ) // 4, (d - 2) % 4
        src = hx.at[s, 3, 0, 0, k] if p == 0 else hy.at[s, 3, 0, 0, k]
        return put(src, rf.at[p, d - 1], "f", (p, d - 1), along_z(d))

    far, near = (2, 3, 4, 5), (6, 7, 1)

    def x_last(s):
        for d in range(2):
            x4(s, d).wait_recv()
        hx[s, 3, 0, 0] = hx[s, 3, 0, 0] + rx4[s, 0] + rx4[s, 1]
        for d in (far, near)[s]:
            last(0, d).start()

    def y_last(s):
        for d in range(2):
            y4(s, d).wait_recv()
        hy[s, 3, 0, 0] = hy[s, 3, 0, 0] + ry4[s, 0] + ry4[s, 1]
        for d in (far, near)[s]:
            last(1, d).start()

    def events(u):
        s, v = u // 4, u % 4
        to_core(u).wait_recv()
        for p in range(2):
            i, h = piece(v, p)
            for g in range(2):
                rows = pl.ds(4 * g, 4)
                hx[s, i, h, g] = own[u % 2, p, rows, :TOP, :LANES] + got[u, p, rows, :TOP, :LANES]
                hy[s, i, h, g] = own[u % 2, p, rows, :TOP, LANES:] + got[u, p, rows, :TOP, LANES:]
                hz[s, v, p, g] = own[u % 2, p, rows, TOP:, :] + got[u, p, rows, TOP:, :]

        @pl.when(v == 0)
        def _():
            for d in range(2):
                x1(s, d).start()
            y_start(s, 0)

        @pl.when(v == 1)
        def _():
            x2(s, 0, 1).start()
            x2(s, 1, 0).start()
            y_start(s, 2)

        @pl.when(v == 2)
        def _():
            y_start(s, 1)

        @pl.when(v == 3)
        def _():
            yd(s).start()
            for d in range(2):
                y2(s, 3, d).start()

        @pl.when(s == 0)
        def _():
            for d in range(2):
                zh(v, d).start()

        @pl.when(s == 1)
        def _():
            for d in range(2):
                z1(v, d).start()
            z_third(v, 1)

        @pl.when(v == 2)
        def _():
            for d in range(2):
                x1(s, d).wait_recv()
                hx[s, 1 + d, d] = hx[s, 1 + d, d] + rx1[s, d]
                x2(s, d, d).start()

        @pl.when((u >= 1) & (u < 5))
        def _():
            z_second(u - 1)

        @pl.when((u >= 2) & (u < 6))
        def _():
            z_third(u - 2, 0)

        @pl.when(v == 1)
        def _():
            y_next(s, 0)

        @pl.when(v == 2)
        def _():
            y_next(s, 2)

        @pl.when(v == 3)
        def _():
            y_next(s, 1)

        @pl.when(u == 5)
        def _():
            x_final(0)
            for d in range(2):
                x3(0, d).start()
            y_final(0, 0)
            for d in range(2):
                y3(0, d).start()

        @pl.when(u == 6)
        def _():
            x_on(0)
            y_final(0, 1)
            y_final(0, 2)
            y_on(0)
            y_final(0, 3)
            z_final(0)
            z5(0).start()

        @pl.when(u == 7)
        def _():
            y_final(1, 0)
            for d in range(2):
                y3(1, d).start()
            z_final(1)

    def turn_units(u, _):
        @pl.when(u < UNITS)
        def _():
            take_columns(u)
            product(1 - core, u // 4, sent, u)

            @pl.when(u == 0)
            def _():
                pl.semaphore_wait(barrier, len(friends))

            to_core(u).start()

        @pl.when(u > 0)
        def _():
            events(u - 1)

        @pl.when(u < UNITS)
        def _():
            product(core, u // 4, own, u % 2)

        return 0

    lax.fori_loop(0, UNITS + 1, turn_units, 0)

    x_last(0)
    y_last(0)
    z_final(2)
    for n in (1, 2):
        z5(n).start()
    x_final(1)
    for d in range(2):
        x3(1, d).start()
    y_final(1, 2)
    y_final(1, 1)
    y_on(1)
    z_final(3)
    for n in range(3):
        z5(n).wait_recv()
    hz[1, 3, 0, :, 2] = hz[1, 3, 0, :, 2] + rz5[0, 0] + rz5[1, 1] + rz5[2, 0]
    hz[1, 3, 1, :, 2] = hz[1, 3, 1, :, 2] + rz5[0, 1] + rz5[1, 0] + rz5[2, 1]
    for n in range(3):
        z7(n).start()
    x_on(1)
    y_final(1, 3)
    y_last(1)
    x_last(1)

    total = hz[1, 3, 0, 0, 2]
    for n in range(3):
        z7(n).wait_recv()
        total = total + rz7[n]
    for p in range(2):
        lanes = slice(p * LANES, (p + 1) * LANES)
        out_ref[TOP:, lanes] = total[:, lanes] / den[p, TOP:]
    for p, mine in ((1, hy), (0, hx)):
        total = mine[1, 3, 0, 0, 2]
        for d in far + near:
            last(p, d).wait_recv()
            total = total + rf[p, d - 1]
        out_ref[:TOP, p * LANES : (p + 1) * LANES] = total / den[p, :TOP]

    def sent_units(u, _):
        to_core(u).wait_send()
        return 0

    def sent_quarters(v, _):
        for d in range(2):
            for sending in (zh, z3, z2, z1):
                sending(v, d).wait_send()
        return 0

    def sent_halves(s, _):
        yd(s).wait_send()
        for d in range(2):
            for sending in (x1, x3, x4, y3, y4):
                sending(s, d).wait_send()
            for h in range(2):
                x2(s, d, h).wait_send()
            for i in range(3):
                y1(s, i, d).wait_send()
            for i in range(4):
                y2(s, i, d).wait_send()
        return 0

    lax.fori_loop(0, UNITS, sent_units, 0)
    lax.fori_loop(0, 4, sent_quarters, 0)
    lax.fori_loop(0, 2, sent_halves, 0)
    for n in range(3):
        z5(n).wait_send()
        z7(n).wait_send()
    for d in range(1, NZ):
        for p in range(2):
            last(p, d).wait_send()


def shards(amplitudes, integrals, occ_energy, virt_energy, outer_energy):
    depth = amplitudes.shape[0] * amplitudes.shape[1]
    t = amplitudes.reshape(depth, amplitudes.shape[2])
    w = integrals.reshape(depth, 4, 4, LANES).transpose(0, 2, 1, 3).reshape(depth * 16, LANES)
    virt = virt_energy.reshape(4, LANES)
    scratch = [pltpu.VMEM(shape, kind) for shape, kind in BUFFERS.values()]
    scratch += [pltpu.SMEM(occ_energy.shape, F32), pltpu.SMEM(outer_energy.shape, F32)]
    scratch += [pltpu.SemaphoreType.DMA((n,)) for n in (8, 8, 3)]
    for shape in SENDS.values():
        scratch += [pltpu.SemaphoreType.DMA(shape)] * 2
    return pl.pallas_call(
        kernel,
        out_shape=jax.ShapeDtypeStruct((ROWS, COLS), F32),
        in_specs=[pl.BlockSpec(memory_space=pl.ANY)] * 5,
        out_specs=pl.BlockSpec(memory_space=pltpu.VMEM),
        scratch_shapes=scratch,
        compiler_params=pltpu.CompilerParams(
            collective_id=0, has_side_effects=True, vmem_limit_bytes=56 * 2**20
        ),
    )(t, w, occ_energy, virt, outer_energy)


def solution(mesh):
    placed = (P("blk", "rep", None), P("blk", "rep", None, None), P(), P(), P())
    return jax.shard_map(
        shards, mesh=mesh, in_specs=placed, out_specs=P("blk", "rep"), check_vma=False
    )
```

time: 600 us -> 56.9 us (0.09)
  waiting for transfers between devices: 325 us -> 0 us
  matrix products: 242 us -> 0 us
  Pallas kernels: 0 us -> 55.4 us
  between operations: 13.4 us -> 0.01 us
  local copies, waits for them, and re-layouts: 11.7 us -> 1.38 us
    ppermute x31 -> x0, waiting for transfers between devices: 293 us -> none  [passed_along(): return lax.ppermute(block, axis, route)]
    dot_general x32 -> x0, matrix products: 242 us -> none  [contract(): lax.dot_general(columns, wmat, (((0,), (0,)), ((), ())), precision=lax.Pr...]
    pallas_call x0 -> x1, Pallas kernels: none -> 55.4 us  [shards(): pl.pallas_call(kernel, out_shape=jax.ShapeDtypeStruct((ROWS, COLS), F32),...]
    reduce_scatter x1 -> x0, waiting for transfers between devices: 31.6 us -> none  [shards(): summed = lax.psum_scatter(carried, 'rep', scatter_dimension=1, tiled=True)]
    unnamed x10 -> x1, local copies, waits for them, and re-layouts: 11.4 us -> 1.38 us
  transfers between devices with their start and end apart: 32 -> 0, of which waited for: 32 -> 0; matrix products, arithmetic and copies ran while one was open for 0% -> 0% of each run, Pallas kernels for 0% -> 0%
where the time goes in v2:
time: 56.9 us; the launch traced here: 56.7 us
  Pallas kernels  55.4 us (97%)
  local copies, waits for them, and re-layouts  1.38 us (2%)
    pallas_call x1, Pallas kernels, shards(): pl.pallas_call(kernel, out_shape=jax.ShapeDtypeStruct((ROWS, COLS), F32),...  55.4 us
    unnamed x1, local copies, waits for them, and re-layouts  1.38 us

profile of v2, /device:TPU:2, one launch (start us, length us, event | category | flops | bytes accessed | tf_op | source)
XLA Modules:
  0.0 56.7 jit_solution(4803146419300347593)
XLA Ops:
  0.0 55.4 %shard_map.55 = f32[32,256]{1,0:T(8,128)} custom-call(f32[1024,1024]{1,0:T(8,128)} %bitcast.8, f32[16384,128]{1,0:T(8,128)} %bitcast.7, f32[64]{0:T(128)} %occ_hbm.1, f32[4,128]{1,0:T(4,128)} %bitcast.9, f32[4]{0:T(128)} %outer_hbm.1), custom_call_target="tpu_custom_call" | custom-call | tf_op jit(solution)/shard_map/pallas_call | solution.py:508
  55.4 1.4 %copy.8 = f32[32,256]{1,0:T(8,128)} copy(f32[32,256]{1,0:T(8,128)} %shard_map.55) | data formatting | bytes 65536

commit v3 on v2

--- a/solution.py
+++ b/solution.py
@@ -20,7 +20,7 @@
     "t_raw": ((8, 1024, LANES), F32),
     "w_raw": ((16384, LANES), F32),
     "tcat": ((2, 2, 256, 3072), BF16),
-    "wcat": ((3072, 2 * COLS), BF16),
+    "wcat": ((4, 3072, 2 * COLS), BF16),
     "own": ((2, 2, 8, ROWS, COLS), F32),
     "sent": ((UNITS, 2, 8, ROWS, COLS), F32),
     "got": ((UNITS, 2, 8, ROWS, COLS), F32),
@@ -29,15 +29,16 @@
     "hz": ((2, 4, 2, 2, 4, LOW, COLS), F32),
     "rx1": ((2, 2, 2, 4, TOP, LANES), F32),
     "rx2": ((2, 2, 2, 2, 4, TOP, LANES), F32),
-    "ry1": ((2, 3, 2, 2, TOP, LANES), F32),
-    "ryd": ((2, 4, TOP, LANES), F32),
+    "ry1": ((2, 2, 2, 2, TOP, LANES), F32),
+    "ryd": ((2, 2, 4, TOP, LANES), F32),
     "ry2": ((2, 4, 2, 4, TOP, LANES), F32),
     "rzh": ((4, 2, 2, LOW, COLS), F32),
     "rz3": ((4, 2, 2, 2, LOW, COLS), F32),
     "rz2": ((4, 2, 2, 2, LOW, COLS), F32),
     "rz1": ((4, 2, 2, 2, LOW, COLS), F32),
-    "rx3": ((2, 2, 2, TOP, LANES), F32),
-    "rx4": ((2, 2, 4, TOP, LANES), F32),
+    "rx3": ((2, 2, TOP, LANES), F32),
+    "rx4": ((2, 4, TOP, LANES), F32),
+    "rx5": ((4, 4, TOP, LANES), F32),
     "ry3": ((2, 2, 2, TOP, LANES), F32),
     "ry4": ((2, 2, 4, TOP, LANES), F32),
     "rz5": ((3, 2, 2, LOW, COLS), F32),
@@ -47,8 +48,8 @@
     "den": ((2, ROWS, LANES), F32),
 }
 SENDS = {
-    "c": (8,), "x1": (2, 2), "x2": (2, 2, 2), "y1": (2, 3, 2), "yd": (2,), "y2": (2, 4, 2),
-    "zh": (4, 2), "z3": (4, 2), "z2": (4, 2), "z1": (4, 2), "x3": (2, 2), "x4": (2, 2),
+    "c": (8,), "x1": (2, 2), "x2": (2, 2, 2), "y1": (2, 2, 2), "yd": (2, 2), "y2": (2, 4, 2),
+    "zh": (4, 2), "z3": (4, 2), "z2": (4, 2), "z1": (4, 2), "x3": (2,), "x4": (2,), "x5": (4, 4),
     "y3": (2, 2), "y4": (2, 2), "z5": (3,), "f": (2, 7), "z7": (3,),
 }
 
@@ -56,7 +57,7 @@
 def kernel(t_hbm, w_hbm, occ_hbm, virt_hbm, outer_hbm, out_ref, *refs):
     names = list(BUFFERS)
     (t_raw, w_raw, tcat, wcat, own, sent, got, hx, hy, hz, rx1, rx2, ry1, ryd, ry2, rzh, rz3, rz2, rz1,
-     rx3, rx4, ry3, ry4, rz5, rf, rz7, virt, den) = refs[: len(names)]
+     rx3, rx4, rx5, ry3, ry4, rz5, rf, rz7, virt, den) = refs[: len(names)]
     occ, outer, load_t, load_w, load_e = refs[len(names) : len(names) + 5]
     left = refs[len(names) + 5 :]
     sems = {name: (left[2 * n], left[2 * n + 1]) for n, name in enumerate(SENDS)}
@@ -75,6 +76,13 @@
     def along_y(d):
         there = (y + d + NY) % NY
         return ((there // 2) * 2 * NZ + z * 2 + core, x * 2 + there % 2)
+
+    def along_yz(dy, dz):
+        there = (y + dy + NY) % NY
+        return (
+            (there // 2) * 2 * NZ + ((z + dz + NZ) % NZ) * 2 + core,
+            x * 2 + there % 2,
+        )
 
     def along_z(d):
         return (y_hi * 2 * NZ + ((z + d + NZ) % NZ) * 2 + core, rep)
@@ -94,6 +102,7 @@
     barrier = pltpu.get_barrier_semaphore()
     friends = [other_core, along_x(1), along_x(-1), along_x(2), along_y(1), along_y(-1), along_y(2)]
     friends += [along_z(d) for d in range(1, NZ)]
+    friends += [along_yz(dy, dz) for dy in (1, -1, 2) for dz in (1, -1, 2, -2)]
     for friend in friends:
         pl.semaphore_signal(barrier, inc=1, device_id=friend, device_id_type=MESH)
 
@@ -144,32 +153,37 @@
     for c in range(2):
         den[c] = (outer[x] + virt[pl.ds(2 * y_lo + c, 1), :]) - pair
 
-    for j in range(8):
-        load_columns(j).wait()
-
     def piece(v, p):
         last = v // 3
         mid = (v + 1) // 2 - 2 * last
         one = mid - (v // 2 - last)
         return mid * (1 + p) + 3 * last, p + one * (1 - 2 * p)
 
-    def take_columns(u):
+    def take_part(v, k, count):
         for p in range(2):
-            i, h = piece(u % 4, p)
+            i, h = piece(v, p)
             ahead = (i // 2) * 3 * (3 - i) + (1 - i // 2) * (2 - i)
             a = (x + ahead) % NX
             b = (y_lo + h) % 2
             for c in range(2):
-                for k in range(0, depth, step):
-                    start = k * 16 + (2 * b + c) * 4 + a
-                    high, low = split(w_raw[pl.ds(start, step, stride=16), :])
-                    lanes = slice(p * COLS + c * LANES, p * COLS + (c + 1) * LANES)
-                    wcat[k : k + step, lanes] = high
-                    wcat[depth + k : depth + k + step, lanes] = high
-                    wcat[2 * depth + k : 2 * depth + k + step, lanes] = low
-
-    def product(which, half, dst, at):
-        value = jnp.dot(tcat[which, half], wcat[...], preferred_element_type=F32)
+                high, low = split(w_raw[pl.ds(k * 16 + (2 * b + c) * 4 + a, count, stride=16), :])
+                lanes = slice(p * COLS + c * LANES, p * COLS + (c + 1) * LANES)
+                for first, value in ((0, high), (depth, high), (2 * depth, low)):
+                    wcat[v, pl.ds(pl.multiple_of(first + k, 128), count), lanes] = value
+
+    def take_first(j, _):
+        load_columns(j).wait()
+        take_part(0, part // 16 * j, part // 16)
+        return 0
+
+    lax.fori_loop(0, 8, take_first, 0)
+
+    def take_columns(v):
+        for k in range(0, depth, step):
+            take_part(v, k, step)
+
+    def product(which, u, dst, at):
+        value = jnp.dot(tcat[which, u // 4], wcat[u % 4], preferred_element_type=F32)
         for p in range(2):
             dst[at, p] = value[:, p * COLS : (p + 1) * COLS].reshape(8, ROWS, COLS)
 
@@ -188,24 +202,32 @@
                 x2(s, d, h).wait_recv()
             hx[s, 3, h] = hx[s, 3, h] + rx2[s, 0, h] + rx2[s, 1, h]
 
-    def x3(s, d):
-        return put(hx.at[s, 3, 0, 1, pl.ds(2 * d, 2)], rx3.at[s, d], "x3", (s, d), along_y(way[d]))
-
-    def x4(s, d):
-        return put(hx.at[s, 3, 1, beside[d]], rx4.at[s, d], "x4", (s, d), along_y(way[d]))
-
-    def x_on(s):
+    def x3(d):
+        return put(hx.at[0, 3, 0, 1, pl.ds(2 * d, 2)], rx3.at[d], "x3", d, along_y(way[d]))
+
+    def x4(d):
+        return put(hx.at[0, 3, 1, beside[d]], rx4.at[d], "x4", d, along_y(way[d]))
+
+    def x_on():
         for d in range(2):
             these = pl.ds(2 * d, 2)
-            x3(s, d).wait_recv()
-            hx[s, 3, 1, beside[d], these] = hx[s, 3, 1, beside[d], these] + rx3[s, d]
-            x4(s, d).start()
+            x3(d).wait_recv()
+            hx[0, 3, 1, beside[d], these] = hx[0, 3, 1, beside[d], these] + rx3[d]
+            x4(d).start()
+
+    def x5(n, k):
+        h, g = ((1, beside[0]), (1, beside[1]), (0, 1), (0, 0))[n]
+        to = along_yz((1, -1, 2, 0)[n], (-2, -1, 0, 1)[k])
+        return put(hx.at[1, 3, h, g, k], rx5.at[n, k], "x5", (n, k), to)
+
+    owners = [(n, k) for n in (2, 0, 1, 3) for k in (0, 1, 3, 2) if (n, k) != (3, 2)]
 
     def y1(s, i, d):
-        return put(hy.at[s, i, 0, 1, pl.ds(2 * d, 2)], ry1.at[s, i, d], "y1", (s, i, d), along_y(way[d]))
-
-    def yd(s):
-        return put(hy.at[s, 3, 0, 1], ryd.at[s], "yd", s, along_y(2))
+        n = i // 2
+        return put(hy.at[s, i, 0, 1, pl.ds(2 * d, 2)], ry1.at[s, n, d], "y1", (s, n, d), along_y(way[d]))
+
+    def yd(s, i):
+        return put(hy.at[s, i, 0, 1], ryd.at[s, i // 2], "yd", (s, i // 2), along_y(2))
 
     def y2(s, i, d):
         return put(hy.at[s, i, 1, beside[d]], ry2.at[s, i, d], "y2", (s, i, d), along_y(way[d]))
@@ -218,16 +240,16 @@
         for d in range(2):
             these = pl.ds(2 * d, 2)
             y1(s, i, d).wait_recv()
-            hy[s, i, 1, beside[d], these] = hy[s, i, 1, beside[d], these] + ry1[s, i, d]
+            hy[s, i, 1, beside[d], these] = hy[s, i, 1, beside[d], these] + ry1[s, i // 2, d]
             y2(s, i, d).start()
 
     def y_final(s, i):
         for d in range(2):
             y2(s, i, d).wait_recv()
         total = hy[s, i, 0, 0] + ry2[s, i, 0] + ry2[s, i, 1]
-        if i == 3:
-            yd(s).wait_recv()
-            total = total + ryd[s]
+        if i % 2 == 1:
+            yd(s, i).wait_recv()
+            total = total + ryd[s, i // 2]
         hy[s, i, 0, 0] = total
 
     def y3(s, d):
@@ -289,11 +311,11 @@
 
     far, near = (2, 3, 4, 5), (6, 7, 1)
 
-    def x_last(s):
-        for d in range(2):
-            x4(s, d).wait_recv()
-        hx[s, 3, 0, 0] = hx[s, 3, 0, 0] + rx4[s, 0] + rx4[s, 1]
-        for d in (far, near)[s]:
+    def x_last():
+        for d in range(2):
+            x4(d).wait_recv()
+        hx[0, 3, 0, 0] = hx[0, 3, 0, 0] + rx4[0] + rx4[1]
+        for d in far:
             last(0, d).start()
 
     def y_last(s):
@@ -325,14 +347,16 @@
             x2(s, 0, 1).start()
             x2(s, 1, 0).start()
             y_start(s, 2)
+            for d in range(2):
+                y2(s, 1, d).start()
 
         @pl.when(v == 2)
         def _():
-            y_start(s, 1)
+            yd(s, 1).start()
 
         @pl.when(v == 3)
         def _():
-            yd(s).start()
+            yd(s, 3).start()
             for d in range(2):
                 y2(s, 3, d).start()
 
@@ -345,7 +369,9 @@
         def _():
             for d in range(2):
                 z1(v, d).start()
-            z_third(v, 1)
+
+    def late_events(u):
+        s, v = u // 4, u % 4
 
         @pl.when(v == 2)
         def _():
@@ -358,9 +384,13 @@
         def _():
             z_second(u - 1)
 
-        @pl.when((u >= 2) & (u < 6))
-        def _():
-            z_third(u - 2, 0)
+        @pl.when(s == 1)
+        def _():
+            z_third(v, 1)
+
+        @pl.when((u >= 3) & (u < 7))
+        def _():
+            z_third(u - 3, 0)
 
         @pl.when(v == 1)
         def _():
@@ -370,26 +400,25 @@
         def _():
             y_next(s, 2)
 
-        @pl.when(v == 3)
-        def _():
-            y_next(s, 1)
+        @pl.when(u == 4)
+        def _():
+            x_final(0)
+            for d in range(2):
+                x3(d).start()
+            y_final(0, 0)
+            for d in range(2):
+                y3(0, d).start()
 
         @pl.when(u == 5)
         def _():
-            x_final(0)
-            for d in range(2):
-                x3(0, d).start()
-            y_final(0, 0)
-            for d in range(2):
-                y3(0, d).start()
-
-        @pl.when(u == 6)
-        def _():
-            x_on(0)
             y_final(0, 1)
             y_final(0, 2)
+            y_final(0, 3)
+
+        @pl.when(u == 6)
+        def _():
+            x_on()
             y_on(0)
-            y_final(0, 3)
             z_final(0)
             z5(0).start()
 
@@ -398,13 +427,11 @@
             y_final(1, 0)
             for d in range(2):
                 y3(1, d).start()
-            z_final(1)
 
     def turn_units(u, _):
         @pl.when(u < UNITS)
         def _():
-            take_columns(u)
-            product(1 - core, u // 4, sent, u)
+            product(1 - core, u, sent, u)
 
             @pl.when(u == 0)
             def _():
@@ -416,25 +443,34 @@
         def _():
             events(u - 1)
 
+        @pl.when(u < 3)
+        def _():
+            take_columns(u + 1)
+
         @pl.when(u < UNITS)
         def _():
-            product(core, u // 4, own, u % 2)
+            product(core, u, own, u % 2)
+
+        @pl.when(u > 0)
+        def _():
+            late_events(u - 1)
 
         return 0
 
     lax.fori_loop(0, UNITS + 1, turn_units, 0)
 
-    x_last(0)
-    y_last(0)
+    x_final(1)
+    for n, k in owners:
+        x5(n, k).start()
+    z_final(1)
     z_final(2)
     for n in (1, 2):
         z5(n).start()
-    x_final(1)
-    for d in range(2):
-        x3(1, d).start()
+    y_final(1, 1)
     y_final(1, 2)
-    y_final(1, 1)
     y_on(1)
+    x_last()
+    y_last(0)
     z_final(3)
     for n in range(3):
         z5(n).wait_recv()
@@ -442,10 +478,8 @@
     hz[1, 3, 1, :, 2] = hz[1, 3, 1, :, 2] + rz5[0, 1] + rz5[1, 0] + rz5[2, 1]
     for n in range(3):
         z7(n).start()
-    x_on(1)
     y_final(1, 3)
     y_last(1)
-    x_last(1)
 
     total = hz[1, 3, 0, 0, 2]
     for n in range(3):
@@ -454,12 +488,19 @@
     for p in range(2):
         lanes = slice(p * LANES, (p + 1) * LANES)
         out_ref[TOP:, lanes] = total[:, lanes] / den[p, TOP:]
-    for p, mine in ((1, hy), (0, hx)):
-        total = mine[1, 3, 0, 0, 2]
-        for d in far + near:
-            last(p, d).wait_recv()
-            total = total + rf[p, d - 1]
-        out_ref[:TOP, p * LANES : (p + 1) * LANES] = total / den[p, :TOP]
+    total = hx[1, 3, 0, 0, 2]
+    for d in far:
+        last(0, d).wait_recv()
+        total = total + rf[0, d - 1]
+    for n, k in owners:
+        x5(n, k).wait_recv()
+        total = total + rx5[n, k]
+    out_ref[:TOP, :LANES] = total / den[0, :TOP]
+    total = hy[1, 3, 0, 0, 2]
+    for d in far + near:
+        last(1, d).wait_recv()
+        total = total + rf[1, d - 1]
+    out_ref[:TOP, LANES:] = total / den[1, :TOP]
 
     def sent_units(u, _):
         to_core(u).wait_send()
@@ -472,13 +513,14 @@
         return 0
 
     def sent_halves(s, _):
-        yd(s).wait_send()
-        for d in range(2):
-            for sending in (x1, x3, x4, y3, y4):
+        yd(s, 1).wait_send()
+        yd(s, 3).wait_send()
+        for d in range(2):
+            for sending in (x1, y3, y4):
                 sending(s, d).wait_send()
             for h in range(2):
                 x2(s, d, h).wait_send()
-            for i in range(3):
+            for i in (0, 2):
                 y1(s, i, d).wait_send()
             for i in range(4):
                 y2(s, i, d).wait_send()
@@ -490,9 +532,15 @@
     for n in range(3):
         z5(n).wait_send()
         z7(n).wait_send()
-    for d in range(1, NZ):
-        for p in range(2):
-            last(p, d).wait_send()
+    for d in range(2):
+        x3(d).wait_send()
+        x4(d).wait_send()
+    for n, k in owners:
+        x5(n, k).wait_send()
+    for d in far:
+        last(0, d).wait_send()
+    for d in far + near:
+        last(1, d).wait_send()
 
 
 def shards(amplitudes, integrals, occ_energy, virt_energy, outer_energy):

time: 56.9 us -> 50.1 us (0.88)
  Pallas kernels: 55.4 us -> 48.5 us
    pallas_call x1, Pallas kernels: 55.4 us -> 48.5 us  [shards(): pl.pallas_call(kernel, out_shape=jax.ShapeDtypeStruct((ROWS, COLS), F32),...]
where the time goes in v3:
time: 50.1 us; the launch traced here: 49.9 us
  Pallas kernels  48.5 us (97%)
  local copies, waits for them, and re-layouts  1.38 us (3%)
    pallas_call x1, Pallas kernels, shards(): pl.pallas_call(kernel, out_shape=jax.ShapeDtypeStruct((ROWS, COLS), F32),...  48.5 us
    unnamed x1, local copies, waits for them, and re-layouts  1.38 us

profile of v3, /device:TPU:2, one launch (start us, length us, event | category | flops | bytes accessed | tf_op | source)
XLA Modules:
  0.0 49.9 jit_solution(14356837369566608045)
XLA Ops:
  0.0 48.5 %shard_map.55 = f32[32,256]{1,0:T(8,128)} custom-call(f32[1024,1024]{1,0:T(8,128)} %bitcast.8, f32[16384,128]{1,0:T(8,128)} %bitcast.7, f32[64]{0:T(128)} %occ_hbm.1, f32[4,128]{1,0:T(4,128)} %bitcast.9, f32[4]{0:T(128)} %outer_hbm.1), custom_call_target="tpu_custom_call" | custom-call | tf_op jit(solution)/shard_map/pallas_call | solution.py:556
  48.6 1.4 %copy.8 = f32[32,256]{1,0:T(8,128)} copy(f32[32,256]{1,0:T(8,128)} %shard_map.55) | data formatting | bytes 65536

commit v4 on v3

--- a/solution.py
+++ b/solution.py
@@ -19,8 +19,8 @@
 BUFFERS = {
     "t_raw": ((8, 1024, LANES), F32),
     "w_raw": ((16384, LANES), F32),
-    "tcat": ((2, 2, 256, 3072), BF16),
-    "wcat": ((4, 3072, 2 * COLS), BF16),
+    "tcat": ((2, 2, 256, 2048), BF16),
+    "wcat": ((4, 2048, 2 * COLS), BF16),
     "own": ((2, 2, 8, ROWS, COLS), F32),
     "sent": ((UNITS, 2, 8, ROWS, COLS), F32),
     "got": ((UNITS, 2, 8, ROWS, COLS), F32),
@@ -88,6 +88,12 @@
         return (y_hi * 2 * NZ + ((z + d + NZ) % NZ) * 2 + core, rep)
 
     other_core = (blk + 1 - 2 * core, rep)
+    at_x = {d: along_x(d) for d in (1, -1, 2)}
+    at_y = {d: along_y(d) for d in (1, -1, 2)}
+    at_z = {d: along_z(d) for d in (1, -1, 2, -2, 3, 4, 5, 6, 7)}
+    at_yz = {(dy, dz): along_yz(dy, dz) for dy in (1, -1, 2) for dz in (1, -1, 2, -2)}
+    at_yz.update({(dy, 0): at_y[dy] for dy in at_y})
+    at_yz.update({(0, dz): at_z[dz] for dz in (1, -1, -2)})
 
     def put(src, dst, name, at, device):
         return pltpu.make_async_remote_copy(
@@ -100,9 +106,9 @@
         )
 
     barrier = pltpu.get_barrier_semaphore()
-    friends = [other_core, along_x(1), along_x(-1), along_x(2), along_y(1), along_y(-1), along_y(2)]
-    friends += [along_z(d) for d in range(1, NZ)]
-    friends += [along_yz(dy, dz) for dy in (1, -1, 2) for dz in (1, -1, 2, -2)]
+    friends = [other_core, at_x[1], at_x[-1], at_x[2], at_y[1], at_y[-1], at_y[2]]
+    friends += [at_z[d] for d in range(1, NZ)]
+    friends += [at_yz[dy, dz] for dy in (1, -1, 2) for dz in (1, -1, 2, -2)]
     for friend in friends:
         pl.semaphore_signal(barrier, inc=1, device_id=friend, device_id_type=MESH)
 
@@ -139,7 +145,6 @@
                 these = slice(32 * m, 32 * m + 32)
                 tcat[m % 2, slot // 4, rows, k : k + step] = high[these]
                 tcat[m % 2, slot // 4, rows, depth + k : depth + k + step] = low[these]
-                tcat[m % 2, slot // 4, rows, 2 * depth + k : 2 * depth + k + step] = high[these]
         return 0
 
     lax.fori_loop(0, 8, turn, 0)
@@ -154,9 +159,10 @@
         den[c] = (outer[x] + virt[pl.ds(2 * y_lo + c, 1), :]) - pair
 
     def piece(v, p):
-        last = v // 3
-        mid = (v + 1) // 2 - 2 * last
-        one = mid - (v // 2 - last)
+        div = (lambda a, b: a // b) if isinstance(v, int) else lax.div
+        last = div(v, 3)
+        mid = div(v + 1, 2) - 2 * last
+        one = mid - (div(v, 2) - last)
         return mid * (1 + p) + 3 * last, p + one * (1 - 2 * p)
 
     def take_part(v, k, count):
@@ -168,22 +174,26 @@
             for c in range(2):
                 high, low = split(w_raw[pl.ds(k * 16 + (2 * b + c) * 4 + a, count, stride=16), :])
                 lanes = slice(p * COLS + c * LANES, p * COLS + (c + 1) * LANES)
-                for first, value in ((0, high), (depth, high), (2 * depth, low)):
+                for first, value in ((0, high), (depth, low)):
                     wcat[v, pl.ds(pl.multiple_of(first + k, 128), count), lanes] = value
 
-    def take_first(j, _):
+    def take_rows(j, _):
         load_columns(j).wait()
-        take_part(0, part // 16 * j, part // 16)
+        for v in range(4):
+            take_part(v, part // 16 * j, part // 16)
         return 0
 
-    lax.fori_loop(0, 8, take_first, 0)
-
-    def take_columns(v):
-        for k in range(0, depth, step):
-            take_part(v, k, step)
+    lax.fori_loop(0, 8, take_rows, 0)
 
     def product(which, u, dst, at):
-        value = jnp.dot(tcat[which, u // 4], wcat[u % 4], preferred_element_type=F32)
+        s, v = lax.div(u, 4), lax.rem(u, 4)
+
+        def dot(a, b):
+            return jnp.dot(
+                tcat[which, s, :, a : a + depth], wcat[v, b : b + depth], preferred_element_type=F32
+            )
+
+        value = dot(0, 0) + dot(depth, 0) + dot(0, depth)
         for p in range(2):
             dst[at, p] = value[:, p * COLS : (p + 1) * COLS].reshape(8, ROWS, COLS)
 
@@ -191,10 +201,16 @@
         return put(sent.at[u], got.at[u], "c", u, other_core)
 
     def x1(s, d):
-        return put(hx.at[s, 0, d], rx1.at[s, d], "x1", (s, d), along_x(way[d]))
+        return put(hx.at[s, 0, d], rx1.at[s, d], "x1", (s, d), at_x[way[d]])
 
     def x2(s, d, h):
-        return put(hx.at[s, 1 + d, h], rx2.at[s, d, h], "x2", (s, d, h), along_x(way[d]))
+        return put(hx.at[s, 1 + d, h], rx2.at[s, d, h], "x2", (s, d, h), at_x[way[d]])
+
+    def x_on_way(s):
+        for d in range(2):
+            x1(s, d).wait_recv()
+            hx[s, 1 + d, d] = hx[s, 1 + d, d] + rx1[s, d]
+            x2(s, d, d).start()
 
     def x_final(s):
         for h in range(2):
@@ -203,10 +219,10 @@
             hx[s, 3, h] = hx[s, 3, h] + rx2[s, 0, h] + rx2[s, 1, h]
 
     def x3(d):
-        return put(hx.at[0, 3, 0, 1, pl.ds(2 * d, 2)], rx3.at[d], "x3", d, along_y(way[d]))
+        return put(hx.at[0, 3, 0, 1, pl.ds(2 * d, 2)], rx3.at[d], "x3", d, at_y[way[d]])
 
     def x4(d):
-        return put(hx.at[0, 3, 1, beside[d]], rx4.at[d], "x4", d, along_y(way[d]))
+        return put(hx.at[0, 3, 1, beside[d]], rx4.at[d], "x4", d, at_y[way[d]])
 
     def x_on():
         for d in range(2):
@@ -217,20 +233,20 @@
 
     def x5(n, k):
         h, g = ((1, beside[0]), (1, beside[1]), (0, 1), (0, 0))[n]
-        to = along_yz((1, -1, 2, 0)[n], (-2, -1, 0, 1)[k])
+        to = at_yz[(1, -1, 2, 0)[n], (-2, -1, 0, 1)[k]]
         return put(hx.at[1, 3, h, g, k], rx5.at[n, k], "x5", (n, k), to)
 
     owners = [(n, k) for n in (2, 0, 1, 3) for k in (0, 1, 3, 2) if (n, k) != (3, 2)]
 
     def y1(s, i, d):
         n = i // 2
-        return put(hy.at[s, i, 0, 1, pl.ds(2 * d, 2)], ry1.at[s, n, d], "y1", (s, n, d), along_y(way[d]))
+        return put(hy.at[s, i, 0, 1, pl.ds(2 * d, 2)], ry1.at[s, n, d], "y1", (s, n, d), at_y[way[d]])
 
     def yd(s, i):
-        return put(hy.at[s, i, 0, 1], ryd.at[s, i // 2], "yd", (s, i // 2), along_y(2))
+        return put(hy.at[s, i, 0, 1], ryd.at[s, i // 2], "yd", (s, i // 2), at_y[2])
 
     def y2(s, i, d):
-        return put(hy.at[s, i, 1, beside[d]], ry2.at[s, i, d], "y2", (s, i, d), along_y(way[d]))
+        return put(hy.at[s, i, 1, beside[d]], ry2.at[s, i, d], "y2", (s, i, d), at_y[way[d]])
 
     def y_start(s, i):
         for d in range(2):
@@ -253,10 +269,10 @@
         hy[s, i, 0, 0] = total
 
     def y3(s, d):
-        return put(hy.at[s, 0, 0, 0, pl.ds(2 * d, 2)], ry3.at[s, d], "y3", (s, d), along_x(way[d]))
+        return put(hy.at[s, 0, 0, 0, pl.ds(2 * d, 2)], ry3.at[s, d], "y3", (s, d), at_x[way[d]])
 
     def y4(s, d):
-        return put(hy.at[s, 1 + d, 0, 0], ry4.at[s, d], "y4", (s, d), along_x(way[d]))
+        return put(hy.at[s, 1 + d, 0, 0], ry4.at[s, d], "y4", (s, d), at_x[way[d]])
 
     def y_on(s):
         for d in range(2):
@@ -266,16 +282,16 @@
             y4(s, d).start()
 
     def zh(v, d):
-        return put(hz.at[0, v, :, d, 2], rzh.at[v, d], "zh", (v, d), along_z(way[d]))
+        return put(hz.at[0, v, :, d, 2], rzh.at[v, d], "zh", (v, d), at_z[way[d]])
 
     def z3(v, d):
-        return put(hz.at[0, v, :, :, 1 + 2 * d], rz3.at[v, d], "z3", (v, d), along_z(way[d]))
+        return put(hz.at[0, v, :, :, 1 + 2 * d], rz3.at[v, d], "z3", (v, d), at_z[way[d]])
 
     def z2(v, d):
-        return put(hz.at[d, v, :, :, 0], rz2.at[v, d], "z2", (v, d), along_z(2 * way[d]))
+        return put(hz.at[d, v, :, :, 0], rz2.at[v, d], "z2", (v, d), at_z[2 * way[d]])
 
     def z1(v, d):
-        return put(hz.at[1, v, :, :, 3 - 2 * d], rz1.at[v, d], "z1", (v, d), along_z(way[d]))
+        return put(hz.at[1, v, :, :, 3 - 2 * d], rz1.at[v, d], "z1", (v, d), at_z[way[d]])
 
     def z_second(v):
         for d in range(2):
@@ -298,16 +314,16 @@
 
     def z5(n):
         src = hz.at[1, 0, :, :, 2] if n == 0 else hz.at[1, 1:3, n - 1, :, 2]
-        return put(src, rz5.at[n], "z5", n, along_x((2, 1, -1)[n]))
+        return put(src, rz5.at[n], "z5", n, at_x[(2, 1, -1)[n]])
 
     def z7(n):
         src = hz.at[1, 3, 1, beside[n], 2] if n < 2 else hz.at[1, 3, 0, 1, 2]
-        return put(src, rz7.at[n], "z7", n, along_y((1, -1, 2)[n]))
+        return put(src, rz7.at[n], "z7", n, at_y[(1, -1, 2)[n]])
 
     def last(p, d):
         s, k = ((d - 2) % NZ) // 4, (d - 2) % 4
         src = hx.at[s, 3, 0, 0, k] if p == 0 else hy.at[s, 3, 0, 0, k]
-        return put(src, rf.at[p, d - 1], "f", (p, d - 1), along_z(d))
+        return put(src, rf.at[p, d - 1], "f", (p, d - 1), at_z[d])
 
     far, near = (2, 3, 4, 5), (6, 7, 1)
 
@@ -326,15 +342,15 @@
             last(1, d).start()
 
     def events(u):
-        s, v = u // 4, u % 4
+        s, v = lax.div(u, 4), lax.rem(u, 4)
         to_core(u).wait_recv()
         for p in range(2):
             i, h = piece(v, p)
             for g in range(2):
                 rows = pl.ds(4 * g, 4)
-                hx[s, i, h, g] = own[u % 2, p, rows, :TOP, :LANES] + got[u, p, rows, :TOP, :LANES]
-                hy[s, i, h, g] = own[u % 2, p, rows, :TOP, LANES:] + got[u, p, rows, :TOP, LANES:]
-                hz[s, v, p, g] = own[u % 2, p, rows, TOP:, :] + got[u, p, rows, TOP:, :]
+                hx[s, i, h, g] = own[lax.rem(u, 2), p, rows, :TOP, :LANES] + got[u, p, rows, :TOP, :LANES]
+                hy[s, i, h, g] = own[lax.rem(u, 2), p, rows, :TOP, LANES:] + got[u, p, rows, :TOP, LANES:]
+                hz[s, v, p, g] = own[lax.rem(u, 2), p, rows, TOP:, :] + got[u, p, rows, TOP:, :]
 
         @pl.when(v == 0)
         def _():
@@ -367,27 +383,26 @@
 
         @pl.when(s == 1)
         def _():
+            z_third(v, 1)
             for d in range(2):
                 z1(v, d).start()
 
+        @pl.when(u == 6)
+        def _():
+            x_on_way(1)
+            y_next(1, 2)
+
     def late_events(u):
-        s, v = u // 4, u % 4
-
-        @pl.when(v == 2)
-        def _():
-            for d in range(2):
-                x1(s, d).wait_recv()
-                hx[s, 1 + d, d] = hx[s, 1 + d, d] + rx1[s, d]
-                x2(s, d, d).start()
+        s, v = lax.div(u, 4), lax.rem(u, 4)
+
+        @pl.when(u == 2)
+        def _():
+            x_on_way(0)
 
         @pl.when((u >= 1) & (u < 5))
         def _():
             z_second(u - 1)
 
-        @pl.when(s == 1)
-        def _():
-            z_third(v, 1)
-
         @pl.when((u >= 3) & (u < 7))
         def _():
             z_third(u - 3, 0)
@@ -396,9 +411,9 @@
         def _():
             y_next(s, 0)
 
-        @pl.when(v == 2)
-        def _():
-            y_next(s, 2)
+        @pl.when(u == 2)
+        def _():
+            y_next(0, 2)
 
         @pl.when(u == 4)
         def _():
@@ -443,13 +458,9 @@
         def _():
             events(u - 1)
 
-        @pl.when(u < 3)
-        def _():
-            take_columns(u + 1)
-
         @pl.when(u < UNITS)
         def _():
-            product(core, u, own, u % 2)
+            product(core, u, own, lax.rem(u, 2))
 
         @pl.when(u > 0)
         def _():

time: 50.1 us -> 48.6 us (0.970)
  Pallas kernels: 48.5 us -> 47 us
    pallas_call x1, Pallas kernels: 48.5 us -> 47 us  [shards(): pl.pallas_call(kernel, out_shape=jax.ShapeDtypeStruct((ROWS, COLS), F32),...]
where the time goes in v4:
time: 48.6 us; the launch traced here: 48.4 us
  Pallas kernels  47 us (97%)
  local copies, waits for them, and re-layouts  1.38 us (3%)
    pallas_call x1, Pallas kernels, shards(): pl.pallas_call(kernel, out_shape=jax.ShapeDtypeStruct((ROWS, COLS), F32),...  47 us
    unnamed x1, local copies, waits for them, and re-layouts  1.38 us

profile of v4, /device:TPU:2, one launch (start us, length us, event | category | flops | bytes accessed | tf_op | source)
XLA Modules:
  0.0 48.4 jit_solution(18209452340949867867)
XLA Ops:
  0.0 47.0 %shard_map.55 = f32[32,256]{1,0:T(8,128)} custom-call(f32[1024,1024]{1,0:T(8,128)} %bitcast.8, f32[16384,128]{1,0:T(8,128)} %bitcast.7, f32[64]{0:T(128)} %occ_hbm.1, f32[4,128]{1,0:T(4,128)} %bitcast.9, f32[4]{0:T(128)} %outer_hbm.1), custom_call_target="tpu_custom_call" | custom-call | tf_op jit(solution)/shard_map/pallas_call | solution.py:567
  47.0 1.4 %copy.8 = f32[32,256]{1,0:T(8,128)} copy(f32[32,256]{1,0:T(8,128)} %shard_map.55) | data formatting | bytes 65536

commit v5 on v4

--- a/solution.py
+++ b/solution.py
@@ -149,15 +149,6 @@
 
     lax.fori_loop(0, 8, turn, 0)
 
-    for load in small:
-        load.wait()
-    at_row = lax.broadcasted_iota(jnp.int32, (ROWS, LANES), 0)
-    pair = jnp.zeros((ROWS, LANES), F32)
-    for r in range(ROWS):
-        pair = jnp.where(at_row == r, occ[blk // 2] + occ[(blk % 2) * ROWS + r], pair)
-    for c in range(2):
-        den[c] = (outer[x] + virt[pl.ds(2 * y_lo + c, 1), :]) - pair
-
     def piece(v, p):
         div = (lambda a, b: a // b) if isinstance(v, int) else lax.div
         last = div(v, 3)
@@ -468,6 +459,30 @@
 
         return 0
 
+    def sent_units(u, _):
+        to_core(u).wait_send()
+        return 0
+
+    def sent_quarters(v, _):
+        for d in range(2):
+            for sending in (zh, z3, z2, z1):
+                sending(v, d).wait_send()
+        return 0
+
+    def sent_halves(s, _):
+        yd(s, 1).wait_send()
+        yd(s, 3).wait_send()
+        for d in range(2):
+            for sending in (x1, y3, y4):
+                sending(s, d).wait_send()
+            for h in range(2):
+                x2(s, d, h).wait_send()
+            for i in (0, 2):
+                y1(s, i, d).wait_send()
+            for i in range(4):
+                y2(s, i, d).wait_send()
+        return 0
+
     lax.fori_loop(0, UNITS + 1, turn_units, 0)
 
     x_final(1)
@@ -477,11 +492,21 @@
     z_final(2)
     for n in (1, 2):
         z5(n).start()
+    for load in small:
+        load.wait()
+    at_row = lax.broadcasted_iota(jnp.int32, (ROWS, LANES), 0)
+    pair = jnp.zeros((ROWS, LANES), F32)
+    for r in range(ROWS):
+        pair = jnp.where(at_row == r, occ[blk // 2] + occ[(blk % 2) * ROWS + r], pair)
+    for c in range(2):
+        den[c] = (outer[x] + virt[pl.ds(2 * y_lo + c, 1), :]) - pair
+    lax.fori_loop(0, UNITS, sent_units, 0)
     y_final(1, 1)
     y_final(1, 2)
     y_on(1)
     x_last()
     y_last(0)
+    lax.fori_loop(0, 4, sent_quarters, 0)
     z_final(3)
     for n in range(3):
         z5(n).wait_recv()
@@ -491,6 +516,12 @@
         z7(n).start()
     y_final(1, 3)
     y_last(1)
+    lax.fori_loop(0, 2, sent_halves, 0)
+    for d in range(2):
+        x3(d).wait_send()
+        x4(d).wait_send()
+    for d in far:
+        last(0, d).wait_send()
 
     total = hz[1, 3, 0, 0, 2]
     for n in range(3):
@@ -513,43 +544,11 @@
         total = total + rf[1, d - 1]
     out_ref[:TOP, LANES:] = total / den[1, :TOP]
 
-    def sent_units(u, _):
-        to_core(u).wait_send()
-        return 0
-
-    def sent_quarters(v, _):
-        for d in range(2):
-            for sending in (zh, z3, z2, z1):
-                sending(v, d).wait_send()
-        return 0
-
-    def sent_halves(s, _):
-        yd(s, 1).wait_send()
-        yd(s, 3).wait_send()
-        for d in range(2):
-            for sending in (x1, y3, y4):
-                sending(s, d).wait_send()
-            for h in range(2):
-                x2(s, d, h).wait_send()
-            for i in (0, 2):
-                y1(s, i, d).wait_send()
-            for i in range(4):
-                y2(s, i, d).wait_send()
-        return 0
-
-    lax.fori_loop(0, UNITS, sent_units, 0)
-    lax.fori_loop(0, 4, sent_quarters, 0)
-    lax.fori_loop(0, 2, sent_halves, 0)
     for n in range(3):
         z5(n).wait_send()
         z7(n).wait_send()
-    for d in range(2):
-        x3(d).wait_send()
-        x4(d).wait_send()
     for n, k in owners:
         x5(n, k).wait_send()
-    for d in far:
-        last(0, d).wait_send()
     for d in far + near:
         last(1, d).wait_send()
 

time: 48.6 us -> 48.4 us (level)
  no operation moved by 1% of the time
where the time goes in v5:
time: 48.4 us; the launch traced here: 48.2 us
  Pallas kernels  46.9 us (97%)
  local copies, waits for them, and re-layouts  1.38 us (3%)
    pallas_call x1, Pallas kernels, shards(): pl.pallas_call(kernel, out_shape=jax.ShapeDtypeStruct((ROWS, COLS), F32),...  46.9 us
    unnamed x1, local copies, waits for them, and re-layouts  1.38 us

profile of v5, /device:TPU:2, one launch (start us, length us, event | category | flops | bytes accessed | tf_op | source)
XLA Modules:
  0.0 48.2 jit_solution(15311183421255557184)
XLA Ops:
  0.0 46.9 %shard_map.55 = f32[32,256]{1,0:T(8,128)} custom-call(f32[1024,1024]{1,0:T(8,128)} %bitcast.8, f32[16384,128]{1,0:T(8,128)} %bitcast.7, f32[64]{0:T(128)} %occ_hbm.1, f32[4,128]{1,0:T(4,128)} %bitcast.9, f32[4]{0:T(128)} %outer_hbm.1), custom_call_target="tpu_custom_call" | custom-call | tf_op jit(solution)/shard_map/pallas_call | solution.py:566
  46.9 1.4 %copy.8 = f32[32,256]{1,0:T(8,128)} copy(f32[32,256]{1,0:T(8,128)} %shard_map.55) | data formatting | bytes 65536
